TPU v7x, 32 devices: a whole 2x2x4 slice. The times are simulated.
32 devices in a mesh: dp: 8 (over z, x), ctx: 4 (over y, core).
Axes of the slice: x: 2, y: 2, z: 4, core: 2. Of those that a mesh axis runs over, the one named last changes fastest.
Arguments:
- hidden: bfloat16 [8, 1024, 4096], P('dp', 'ctx'), may hold values from -6 to 6
- segments: int32 [8, 1024], P('dp', 'ctx'), may hold values from 0 to 7, as said below
- gain: float32 [4096], replicated, may hold values from 0.25 to 1.75
- inv_temp: float32 [], replicated, may hold values from 20 to 50
- positives: int32 [64], P(('dp', 'ctx')), may hold values from 0 to 63, as said below
Outputs:
- grad_hidden: bfloat16 [8, 1024, 4096], P('dp', 'ctx')
- grad_gain: float32 [4096], replicated
- loss: float32 [], replicated
Inputs may be any that keep to these rules, and one draw needn't show every extreme that they name: `segments`: in each sequence the document numbers never fall along positions and every document has one position or more; document 0 covers more than half of the sequence's positions. `positives`: no document is its own positive.
All inputs are finite; a program needn't handle non-finite values.
Results may differ from a plain program's by a relative error of at most 0.0053.
Values may be sent and summed in bfloat16 or wider, within the bound.
No kernel may reach another device: no remote copies, remote signals or barrier semaphores. Data moves between devices by JAX's collectives and lax.ppermute only.
A program may use at most 64 MiB of HBM per device.

v0:
```python
import jax
import jax.numpy as jnp
from jax import lax
from jax.sharding import PartitionSpec as P

DOCS_DEV = 2


def normalize_docs(pooled_totals, counts):
    pooled = pooled_totals / counts[:, None]
    rnorm = lax.rsqrt(jnp.sum(pooled * pooled, axis=-1, keepdims=True) + 1e-06)
    return (pooled * rnorm, rnorm)


def body(hidden, segments, gain, inv_temp, positives):
    states = hidden[0].astype(jnp.float32)
    scale_t = lax.rsqrt(jnp.mean(states * states, axis=-1, keepdims=True) + 1e-06)
    normalized_rows = states * scale_t * gain
    ctx_count = lax.axis_size("ctx")
    seq_docs = DOCS_DEV * ctx_count
    document_indicator = (
        segments[0][:, None] == jnp.arange(seq_docs, dtype=jnp.int32)[None, :]
    ).astype(jnp.float32)
    pooled_totals = lax.dot_general(
        document_indicator,
        normalized_rows,
        (((0,), (0,)), ((), ())),
        precision=lax.Precision.HIGHEST,
    )
    counts = jnp.sum(document_indicator, axis=0)
    ctx_rank = lax.axis_index("ctx")
    own_start = ctx_rank * DOCS_DEV
    sequence_pooled_sums, seq_counts = lax.psum((pooled_totals, counts), "ctx")
    seq_emb_f, seq_rnorm = normalize_docs(sequence_pooled_sums, seq_counts)
    seq_emb = seq_emb_f.astype(jnp.bfloat16)
    emb_all = lax.all_gather(seq_emb, "dp", axis=0, tiled=True)
    emb_f = lax.dynamic_slice_in_dim(seq_emb_f, own_start, DOCS_DEV, 0)
    rnorm = lax.dynamic_slice_in_dim(seq_rnorm, own_start, DOCS_DEV, 0)
    emb_own = lax.dynamic_slice_in_dim(seq_emb, own_start, DOCS_DEV, 0)
    own_counts = lax.dynamic_slice_in_dim(seq_counts, own_start, DOCS_DEV, 0)
    all_docs = emb_all.shape[0]
    row_first = (lax.axis_index("dp") * ctx_count + ctx_rank) * DOCS_DEV
    logits = (
        lax.dot_general(
            emb_own, emb_all, (((1,), (1,)), ((), ())), preferred_element_type=jnp.float32
        )
        * inv_temp
    )
    columns = jnp.arange(all_docs, dtype=jnp.int32)[None, :]
    own_rows = row_first + jnp.arange(DOCS_DEV, dtype=jnp.int32)[:, None]
    pos_mask = (columns == positives[:, None]).astype(jnp.float32)
    logits = jnp.where(columns == own_rows, -1e30, logits)
    top = jnp.max(logits, axis=1, keepdims=True)
    expo = jnp.exp(logits - top)
    total = jnp.sum(expo, axis=1, keepdims=True)
    lse = top[:, 0] + jnp.log(total[:, 0])
    loss_local = jnp.sum(lse - jnp.sum(pos_mask * logits, axis=1)) / all_docs
    gmat = ((expo / total - pos_mask) * (inv_temp / all_docs)).astype(jnp.bfloat16)
    row_grad = jnp.dot(gmat, emb_all, preferred_element_type=jnp.float32)
    grad_rows = lax.all_gather(gmat, ("dp", "ctx"), axis=0, tiled=True)
    grad_cols = lax.dynamic_slice_in_dim(grad_rows, row_first, DOCS_DEV, 1)
    col_grad = lax.dot_general(
        grad_cols, emb_all, (((0,), (0,)), ((), ())), preferred_element_type=jnp.float32
    )
    demb = row_grad + col_grad
    dpool = rnorm * (demb - emb_f * jnp.sum(emb_f * demb, axis=-1, keepdims=True))
    dsum_own = dpool / own_counts[:, None]
    dsum_seq = lax.all_gather(dsum_own, "ctx", axis=0, tiled=True)
    normalized_gradient = jnp.dot(document_indicator, dsum_seq, precision=lax.Precision.HIGHEST)
    gain_local = jnp.sum(normalized_gradient * states * scale_t, axis=0)
    grad_gain, loss = lax.psum((gain_local, loss_local), ("dp", "ctx"))
    grad_out = normalized_gradient * gain
    inner = jnp.mean(grad_out * states, axis=-1, keepdims=True)
    grad_hidden = (scale_t * grad_out - states * scale_t**3 * inner).astype(jnp.bfloat16)
    return (grad_hidden[None], grad_gain, loss)


def solution(mesh):
    return jax.shard_map(
        body,
        mesh=mesh,
        in_specs=(P("dp", "ctx", None), P("dp", "ctx"), P(), P(), P(("dp", "ctx"))),
        out_specs=(P("dp", "ctx", None), P(), P()),
        check_vma=False,
    )
```

profile of v0, /device:TPU:0, one launch (start us, length us, event | category | flops | bytes accessed | tf_op | source)
XLA Modules:
  0.0 183.4 jit_solution(8204630516442707392)
XLA Ops:
  7.2 0.0 copy-start.3
  7.2 0.0 copy-start.2
  7.2 0.0 all-reduce.3.cloned.1.call-start
  7.2 2.1 %fusion = f32[256]{0:T(256)S(1)} fusion(bf16[1,256,4096]{2,1,0:T(8,128)(2,1)} %param.5), kind=kLoop, calls=%fused_computation.6 | loop fusion | flops 3145472 | bytes 2098176 | tf_op jit(solution)/shard_map/reduce_sum | solution.py:17
  9.3 0.0 copy-start
  9.3 0.0 copy-start.1
  9.4 4.3 %fusion.2 = f32[8,4096]{1,0:T(8,128)} fusion(bf16[1,256,4096]{2,1,0:T(8,128)(2,1)} %param.5, f32[4096]{0:T(1024)} %param.7, f32[256]{0:T(256)S(1)} %get-tuple-element.12, s32[256]{0:T(256)} %bitcast.24), kind=kOutput, calls=%fused_computation.8 | convolution fusion | flops 103811072 | bytes 2246656 | tf_op jit(solution)/shard_map/dot_general | solution.py:24
  13.6 0.0 all-reduce.3.cloned.1.call-update
  13.6 0.0 copy-done.3
  13.7 0.1 convert_reduce_fusion
  14.4 8.4 %psum.29 = f32[8]{0:T(128)S(1)} all-reduce(f32[8]{0:T(128)S(1)} %convert_reduce_fusion), channel_id=1, replica_groups=mesh['dp'=8,'ctx'=4] {'ctx'}, use_global_device_ids=true, to_apply=%region_3.0 | all-reduce | flops 8 | bytes 64 | tf_op jit(solution)/shard_map/psum | solution.py:33
  22.8 0.1 dynamic_slice.16
  22.9 25.0 %all-reduce.3.cloned.1.call-done = f32[8,4096]{1,0:T(8,128)} async-done(((f32[8,4096]{1,0:T(8,128)}), f32[8,4096]{1,0:T(8,128)}) %all-reduce.3.cloned.1.call-update) | async-done | bytes 131088 | tf_op jit(solution)/shard_map/psum | solution.py:33
  47.9 1.1 multiply_reduce_fusion
  49.0 0.1 dynamic-slice.3
  49.1 1.0 fusion.23
  50.1 31.4 %all_gather.9 = bf16[64,4096]{1,0:T(8,128)(2,1)S(1)} all-gather(bf16[8,4096]{1,0:T(8,128)(2,1)S(1)} %get-tuple-element.9), channel_id=1, replica_groups=mesh['dp'=8,'ctx'=4] {'dp'}, dimensions={0}, use_global_device_ids=true | all-gather | bytes 589824 | tf_op jit(solution)/shard_map/all_gather | solution.py:36
  81.5 0.4 fusion.24
  81.8 0.0 copy-done.2
  81.8 0.2 select_reduce_fusion
  82.1 0.1 fusion.31
  82.1 0.3 fusion.25
  82.4 0.6 subtract_reduce_fusion
  83.7 40.2 %all-gather = bf16[32,2,64]{2,1,0:T(2,128)(2,1)S(1)} all-gather(bf16[1,2,64]{2,1,0:T(2,128)(2,1)S(1)} %fusion.31), channel_id=1, replica_groups=mesh['dp'=8,'ctx'=4] {'dp','ctx'}, dimensions={0}, use_global_device_ids=true | all-gather | bytes 8448 | tf_op jit(solution)/shard_map/all_gather | solution.py:60
  123.9 0.4 multiply_reduce_fusion.1
  124.3 0.1 divide_bitcast_fusion
  124.4 5.4 %all-gather.1 = f32[4,2,4096]{2,1,0:T(2,128)S(1)} all-gather(f32[1,2,4096]{2,1,0:T(2,128)S(1)} %divide_bitcast_fusion), channel_id=1, replica_groups=mesh['dp'=8,'ctx'=4] {'ctx'}, dimensions={0}, use_global_device_ids=true | all-gather | bytes 163840 | tf_op jit(solution)/shard_map/all_gather | solution.py:68
  129.8 0.1 reshape.60
  129.9 0.0 copy-done
  129.9 0.0 copy-done.1
  129.9 4.6 %fusion.9 = (f32[4096]{0:T(1024)S(1)}, f32[256]{0:T(256)S(1)}, f32[256,4096]{1,0:T(8,128)}) fusion(bf16[1,256,4096]{2,1,0:T(8,128)(2,1)S(1)} %copy-done, f32[256]{0:T(256)S(1)} %get-tuple-element.12, f32[4096]{0:T(1024)S(1)} %copy-done.1, f32[8,4096]{1,0:T(8,128)S(1)} %reshape.60, s32[256]{0:T(256)S(1)} %bitcast.26), kind=kOutput, calls=%fused_computation.14 | convolution fusion | flops 108001024 | bytes 6458368 | tf_op jit(solution)/shard_map/dot_general | solution.py:69
  134.5 37.2 %all-reduce = (f32[4096]{0:T(1024)}, f32[]{:T(128)}) all-reduce(f32[4096]{0:T(1024)S(1)} %get-tuple-element.3, f32[]{:T(128)S(6)} %div.45), channel_id=1, replica_groups=mesh['dp'=8,'ctx'=4] {'dp','ctx'}, use_global_device_ids=true, to_apply=%region_10.11 | all-reduce | flops 4097 | bytes 32776 | tf_op jit(solution)/shard_map/psum | solution.py:71
  171.7 4.9 %fusion.10 = bf16[1,256,4096]{2,1,0:T(8,128)(2,1)} fusion(f32[256,4096]{1,0:T(8,128)} %get-tuple-element.17, bf16[1,256,4096]{2,1,0:T(8,128)(2,1)S(1)} %copy-done, f32[256]{0:T(256)S(1)} %broadcast_multiply_fusion.1, f32[256]{0:T(256)S(1)} %get-tuple-element.11, f32[4096]{0:T(1024)S(1)} %copy-done.1, f32[256]{0:T(256)S(1)} %get-tuple-element.12), kind=kLoop, calls=%fused_computation.15 | loop fusion | flops 7340032 | bytes 8408064 | tf_op jit(solution)/shard_map/broadcast_in_dim | solution.py:75
  (4 shorter events, 0.0 us)
Async XLA Ops:
  7.2 6.5 %copy-start.3 = (s32[1,256]{1,0:T(1,128)S(1)}, s32[1,256]{1,0:T(1,128)}, u32[]{:S(2)}) copy-start(s32[1,256]{1,0:T(1,128)} %param.6) | copy-start | bytes 3076
  7.2 74.7 %copy-start.2 = (s32[2]{0:T(128)S(1)}, s32[2]{0:T(128)}, u32[]{:S(2)}) copy-start(s32[2]{0:T(128)} %param.9) | copy-start | bytes 28
  7.2 40.7 %all-reduce.3.cloned.1.call-start = ((), (), s32[]{:S(2)}) async-start(), calls=%async_computation | async-start | bytes 262144 | tf_op jit(solution)/shard_map/psum | solution.py:33
  9.3 120.6 %copy-start = (bf16[1,256,4096]{2,1,0:T(8,128)(2,1)S(1)}, bf16[1,256,4096]{2,1,0:T(8,128)(2,1)}, u32[]{:S(2)}) copy-start(bf16[1,256,4096]{2,1,0:T(8,128)(2,1)} %param.5) | copy-start | bytes 6291460
  9.3 120.6 %copy-start.1 = (f32[4096]{0:T(1024)S(1)}, f32[4096]{0:T(1024)}, u32[]{:S(2)}) copy-start(f32[4096]{0:T(1024)} %param.7) | copy-start | bytes 49156
Sparse Core Ops, SparseCore 0:
  13.8 34.0 all-reduce.2
where the time goes:
time: 185 us; the launch traced here: 183 us
  blocking collectives  123 us (66%)
  waiting for transfers between devices  25 us (14%)
  between operations  15.4 us (8%)
  other arithmetic  10.2 us (6%)
  matrix products  9.88 us (5%)
    all_gather x1, blocking collectives, body(): grad_rows = lax.all_gather(gmat, ('dp', 'ctx'), axis=0, tiled=True)  40.2 us
    psum x1, blocking collectives, body(): grad_gain, loss = lax.psum((gain_local, loss_local), ('dp', 'ctx'))  37.2 us
    all_gather x1, blocking collectives, body(): emb_all = lax.all_gather(seq_emb, 'dp', axis=0, tiled=True)  31.4 us
    psum x1, waiting for transfers between devices, body(): sequence_pooled_sums, seq_counts = lax.psum((pooled_totals, counts), 'ctx')  25 us
    psum x1, blocking collectives, body(): sequence_pooled_sums, seq_counts = lax.psum((pooled_totals, counts), 'ctx')  8.37 us
    all_gather x1, blocking collectives, body(): dsum_seq = lax.all_gather(dsum_own, 'ctx', axis=0, tiled=True)  5.43 us
    broadcast_in_dim x1, other arithmetic, body(): return (grad_hidden[None], grad_gain, loss)  4.87 us
    dot_general x1, matrix products, body(): jnp.dot(document_indicator, dsum_seq, precision=lax.Precision.HIGHEST)  4.58 us
  transfers between devices with their start and end apart: 1, of which 1 were waited for; matrix products, arithmetic and copies ran while one was open for 0% of the time, Pallas kernels for 0%

commit v1 on v0

v1 whole, which is shorter than its diff:
```python
import functools

import jax
import jax.numpy as jnp
from jax import lax
from jax.experimental import pallas as pl
from jax.experimental.pallas import tpu as pltpu
from jax.sharding import PartitionSpec as P

EPS = 1e-06
EXTRA = 128
BASE = 16
POOL_ROWS = 64
OUT_ROWS = 64
LANES = 256
BOTH = ("dp", "ctx")
VMEM_LIMIT = 32 * 1024 * 1024
F32, BF16 = jnp.float32, jnp.bfloat16


def _pieces(size, want):
    return want if size % want == 0 else size


def _spare_rows(docs):
    return -(-3 * docs // 16) * 16


def pool_kernel(docs, positives_ref, place_ref, segments_ref, gain_ref, hidden_ref, part_ref, weights_ref, square_ref, held, acc, sems):
    tokens, width = held.shape
    rows = _pieces(tokens, POOL_ROWS)
    copies = []
    for at in range(0, tokens, rows):
        copy = pltpu.make_async_copy(hidden_ref.at[0, pl.ds(at, rows)], held.at[pl.ds(at, rows)], sems.at[at // rows])
        copy.start()
        copies.append(copy)
    segments = segments_ref[...]
    slot = lax.broadcasted_iota(jnp.int32, (128, tokens), 0)
    member_t = jnp.where((slot < 3 * docs) & (slot % docs == segments), 1.0, 0.0)
    member = jnp.transpose(member_t)
    lane = lax.broadcasted_iota(jnp.int32, (rows, 128), 1)
    for step, copy in enumerate(copies):
        at = step * rows
        copy.wait()
        states = held[at : at + rows, :].astype(F32)
        mean = jnp.sum(states * states, axis=1, keepdims=True) / width
        scale = lax.rsqrt(mean + EPS)
        weight = member[at : at + rows, :] * scale
        high = weight.astype(BF16).astype(F32)
        weight = jnp.where(lane < 2 * docs, high, weight - high)
        weights_ref[at : at + rows, :] = weight.astype(BF16)
        square_ref[at : at + rows, :] = jnp.broadcast_to(scale * scale / width, (rows, 128))
        spread = jnp.transpose(weight)[docs : 3 * docs, :].astype(BF16)
        part = lax.dot_general(spread, held[at : at + rows, :], (((1,), (0,)), ((), ())), preferred_element_type=F32)
        if step == 0:
            acc[...] = part
        else:
            acc[...] += part
    part_ref[:, :width] = (acc[:docs, :] + acc[docs:, :]) * gain_ref[...]
    count = jnp.sum(member_t[:docs, :], axis=1, keepdims=True).astype(jnp.int32)
    row = lax.broadcasted_iota(jnp.int32, (docs, EXTRA), 0)
    lane = lax.broadcasted_iota(jnp.int32, (docs, EXTRA), 1)
    own = positives_ref.shape[0]
    positive = jnp.zeros((docs, EXTRA), jnp.int32)
    for i in range(own):
        positive = jnp.where(row == place_ref[0] * own + i, positives_ref[i], positive)
    digits = jnp.where(lane == 0, count // BASE, 0)
    digits = jnp.where(lane == 1, count % BASE, digits)
    digits = jnp.where(lane == 2, positive // BASE, digits)
    digits = jnp.where(lane == 3, positive % BASE, digits)
    part_ref[:, width:] = digits.astype(F32)


def loss_kernel(docs, n_blocks, temp_ref, place_ref, *refs):
    blocks = refs[:n_blocks]
    gain_ref, weights_ref, square_ref, hidden_ref, grad_hidden_ref, grad_gain_ref, loss_ref, emb, spare, own_rows, held, out, sems = refs[n_blocks:]
    tokens, width = held.shape
    n = emb.shape[0]
    group = blocks[0].shape[0]
    load = pltpu.make_async_copy(hidden_ref.at[0], held, sems.at[0])
    load.start()
    for i, block in enumerate(blocks):
        emb[pl.ds(pl.multiple_of(place_ref[1 + i] * group, group), group), :] = block[...]
    inv_temp = temp_ref[0]
    gram = lax.dot_general(emb[:, :width], emb[:, :width], (((1,), (1,)), ((), ())), preferred_element_type=F32)
    digits = emb[:, width:].astype(F32)
    digits_t = jnp.transpose(digits)
    count_c = digits[:, 0:1] * BASE + digits[:, 1:2]
    count_r = digits_t[0:1, :] * BASE + digits_t[1:2, :]
    positive = (digits[:, 2:3] * BASE + digits[:, 3:4]).astype(jnp.int32)
    row = lax.broadcasted_iota(jnp.int32, (n, n), 0)
    column = lax.broadcasted_iota(jnp.int32, (n, n), 1)
    same = row == column
    squares = jnp.where(same, gram, 0.0)
    norm_c = lax.rsqrt(jnp.sum(squares, axis=1, keepdims=True) + EPS * count_c * count_c)
    norm_r = lax.rsqrt(jnp.sum(squares, axis=0, keepdims=True) + EPS * count_r * count_r)
    cosine = gram * norm_c * norm_r
    logits = jnp.where(same, -1e30, cosine * inv_temp)
    top = jnp.max(logits, axis=1, keepdims=True)
    expo = jnp.exp(logits - top)
    total = jnp.sum(expo, axis=1, keepdims=True)
    pos_mask = jnp.where(column == positive, 1.0, 0.0)
    terms = top + jnp.log(total) - jnp.sum(pos_mask * logits, axis=1, keepdims=True)
    loss_ref[...] = jnp.sum(terms, axis=0, keepdims=True) / n
    gmat = ((expo / total - pos_mask) * (inv_temp / n)).astype(BF16).astype(F32)
    both = gmat + jnp.transpose(gmat)
    along = jnp.sum(both * cosine, axis=1, keepdims=True)
    mix = norm_c * (both * norm_r - jnp.where(same, along * norm_r, 0.0))
    own_rows[...] = mix
    own = own_rows[pl.ds(pl.multiple_of(place_ref[0] * docs, docs), docs), :]
    mix_high, own_high = mix.astype(BF16), own.astype(BF16)
    mix_low, own_low = (mix - mix_high.astype(F32)).astype(BF16), (own - own_high.astype(F32)).astype(BF16)
    stack = jnp.concatenate([mix_high.astype(F32), mix_low.astype(F32), own_high.astype(F32), own_low.astype(F32)], axis=0).astype(BF16)
    load.wait()
    lanes = _pieces(width, LANES)
    spare_rows = spare.shape[0]
    inner = jnp.zeros((tokens, spare_rows), F32)
    for at in range(0, width, lanes):
        sums = emb[:, at : at + lanes]
        gain = gain_ref[:, at : at + lanes]
        grads = jnp.dot(stack, sums, preferred_element_type=F32)
        dsum = grads[:n, :] + grads[n : 2 * n, :]
        grad_gain_ref[:, at : at + lanes] = jnp.sum(dsum * sums.astype(F32), axis=0, keepdims=True) / gain
        mine = (grads[2 * n : 2 * n + docs, :] + grads[2 * n + docs :, :]) * gain
        high = mine.astype(BF16).astype(F32)
        parts = [high, mine - high, high]
        if spare_rows > 3 * docs:
            parts.append(jnp.zeros((spare_rows - 3 * docs, lanes), F32))
        part = jnp.concatenate(parts, axis=0).astype(BF16)
        spare[:, at : at + lanes] = part
        inner += lax.dot_general(held[:, at : at + lanes], part, (((1,), (1,)), ((), ())), preferred_element_type=F32)
    weights = weights_ref[:, :spare_rows]
    pull = jnp.sum(weights.astype(F32) * inner, axis=1, keepdims=True) * square_ref[:, 0:1]
    rows = _pieces(tokens, OUT_ROWS)
    copies = []
    for at in range(0, tokens, rows):
        for left in range(0, width, lanes):
            spread = jnp.dot(weights[at : at + rows, :], spare[:, left : left + lanes], preferred_element_type=F32)
            states = held[at : at + rows, left : left + lanes].astype(F32)
            out[at : at + rows, left : left + lanes] = (spread - states * pull[at : at + rows, :]).astype(BF16)
        copy = pltpu.make_async_copy(out.at[pl.ds(at, rows)], grad_hidden_ref.at[0, pl.ds(at, rows)], sems.at[1 + at // rows])
        copy.start()
        copies.append(copy)
    for copy in copies:
        copy.wait()


def _vmem():
    return pl.BlockSpec(memory_space=pltpu.VMEM)


def _smem():
    return pl.BlockSpec(memory_space=pltpu.SMEM)


def _any():
    return pl.BlockSpec(memory_space=pl.ANY)


def tree_sum(values):
    while len(values) > 1:
        values = [values[i] + values[i + 1] for i in range(0, len(values), 2)]
    return values[0]


def body(dp, ctx, hidden, segments, gain, inv_temp, positives):
    _, tokens, width = hidden.shape
    docs = positives.shape[0] * ctx
    n = docs * dp
    rows_out, rows_in = _pieces(tokens, OUT_ROWS), _pieces(tokens, POOL_ROWS)
    d, c = lax.axis_index("dp"), lax.axis_index("ctx")
    core = lax.rem(c, 2)
    gain = gain.reshape(1, width)

    def move(x, to):
        return lax.ppermute(x, BOTH, [(i * ctx + j, to(i, j)[0] * ctx + to(i, j)[1]) for i in range(dp) for j in range(ctx)])

    part, weights, square = pl.pallas_call(
        functools.partial(pool_kernel, docs),
        out_shape=(
            jax.ShapeDtypeStruct((docs, width + EXTRA), F32),
            jax.ShapeDtypeStruct((tokens, 128), BF16),
            jax.ShapeDtypeStruct((tokens, 128), F32),
        ),
        in_specs=[_smem(), _smem(), _vmem(), _vmem(), _any()],
        out_specs=(_vmem(), _vmem(), _vmem()),
        scratch_shapes=[
            pltpu.VMEM((tokens, width), BF16),
            pltpu.VMEM((2 * docs, width), F32),
            pltpu.SemaphoreType.DMA((tokens // rows_in,)),
        ],
        compiler_params=pltpu.CompilerParams(vmem_limit_bytes=VMEM_LIMIT),
        name="pool",
    )(positives, c.reshape(1), segments, gain, hidden)

    chip = (part + move(part, lambda i, j: (i, j ^ 1))).astype(BF16)
    found = {}
    for dx in range(2):
        for dy in range(ctx // 2):
            found[dx, dy] = chip if (dx, dy) == (0, 0) else move(chip, lambda i, j: (i ^ dx, j ^ (2 * dy)))
    here, there = (tree_sum([found[dx, dy].astype(F32) for dy in range(ctx // 2)]).astype(BF16) for dx in range(2))
    odd = lax.rem(d, 2) == 1
    pair = jnp.concatenate([jnp.where(odd, there, here), jnp.where(odd, here, there)], axis=0)

    groups = dp // 2
    g = d // 2
    blocks, places = [pair], [g]

    def swap(x):
        return move(x, lambda i, j: (i, j ^ 1))

    for k in range(1, groups - 1, 2):
        mine = move(pair, lambda i, j: (i ^ (2 * (k + j % 2)), j))
        blocks += [mine, swap(mine)]
        places += [g ^ (k + core), g ^ (k + 1 - core)]
    if groups > 1:
        half = move(jnp.where(core == 0, pair[:docs], pair[docs:]), lambda i, j: (i ^ (2 * (groups - 1)), j))
        other = swap(half)
        blocks.append(jnp.concatenate([jnp.where(core == 0, half, other), jnp.where(core == 0, other, half)], axis=0))
        places.append(g ^ (groups - 1))

    place = jnp.stack([d] + places).astype(jnp.int32)
    grad_hidden, grad_gain, loss = pl.pallas_call(
        functools.partial(loss_kernel, docs, len(blocks)),
        out_shape=(
            jax.ShapeDtypeStruct((1, tokens, width), BF16),
            jax.ShapeDtypeStruct((1, width), F32),
            jax.ShapeDtypeStruct((1, 1), F32),
        ),
        in_specs=[_smem(), _smem()] + [_vmem()] * (len(blocks) + 3) + [_any()],
        out_specs=(_any(), _vmem(), _vmem()),
        scratch_shapes=[
            pltpu.VMEM((n, width + EXTRA), BF16),
            pltpu.VMEM((_spare_rows(docs), width), BF16),
            pltpu.VMEM((n, n), F32),
            pltpu.VMEM((tokens, width), BF16),
            pltpu.VMEM((tokens, width), BF16),
            pltpu.SemaphoreType.DMA((1 + tokens // rows_out,)),
        ],
        compiler_params=pltpu.CompilerParams(vmem_limit_bytes=VMEM_LIMIT),
        name="loss",
    )(inv_temp.reshape(1), place, *blocks, gain, weights, square, hidden)
    return grad_hidden, grad_gain.reshape(width), loss.reshape(())


def solution(mesh):
    return jax.shard_map(
        functools.partial(body, mesh.shape["dp"], mesh.shape["ctx"]),
        mesh=mesh,
        in_specs=(P("dp", "ctx", None), P("dp", "ctx"), P(), P(), P(("dp", "ctx"))),
        out_specs=(P("dp", "ctx", None), P(), P()),
        check_vma=False,
    )
```

time: 185 us -> 33.6 us (0.18)
  blocking collectives: 123 us -> 0 us
  waiting for transfers between devices: 25 us -> 10.7 us
  between operations: 15.4 us -> 1.33 us
  other arithmetic: 10.2 us -> 0.12 us
  matrix products: 9.88 us -> 0 us
  starting transfers between devices: 0.04 us -> 9.63 us
  Pallas kernels: 0 us -> 7.85 us
  local copies, waits for them, and re-layouts: 0.27 us -> 3.73 us
    all_gather x3 -> x0, blocking collectives: 77 us -> none  [the longest x1 40.2 us: body(): grad_rows = lax.all_gather(gmat, ('dp', 'ctx'), axis=0, tiled=True)]
    psum x2 -> x0, blocking collectives: 45.5 us -> none  [the longest x1 37.2 us: body(): grad_gain, loss = lax.psum((gain_local, loss_local), ('dp', 'ctx'))]
    psum x1 -> x0, waiting for transfers between devices: 25 us -> none  [body(): sequence_pooled_sums, seq_counts = lax.psum((pooled_totals, counts), 'ctx')]
    ppermute x0 -> x8, waiting for transfers between devices: none -> 10.7 us  [move(): lax.ppermute(x, BOTH, [(i * ctx + j, to(i, j)[0] * ctx + to(i, j)[1]) for...]
    dot_general x5 -> x0, matrix products: 9.88 us -> none  [the longest x1 4.58 us: body(): jnp.dot(document_indicator, dsum_seq, precision=lax.Precision.HIGHEST)]
    ppermute x0 -> x8, starting transfers between devices: none -> 9.63 us  [move(): lax.ppermute(x, BOTH, [(i * ctx + j, to(i, j)[0] * ctx + to(i, j)[1]) for...]
    pallas_call x0 -> x2, Pallas kernels: none -> 7.85 us  [the longest x1 5.58 us: body(): pl.pallas_call(functools.partial(loss_kernel, docs, len(blocks)), out_sha...]
    broadcast_in_dim x1 -> x0, other arithmetic: 4.87 us -> none  [body(): return (grad_hidden[None], grad_gain, loss)]
  transfers between devices with their start and end apart: 1 -> 8, of which waited for: 1 -> 5; matrix products, arithmetic and copies ran while one was open for 0% -> 0% of each run, Pallas kernels for 0% -> 0%
where the time goes in v1:
time: 33.6 us; the launch traced here: 33.3 us
  waiting for transfers between devices  10.7 us (32%)
  starting transfers between devices  9.63 us (29%)
  Pallas kernels  7.85 us (23%)
  local copies, waits for them, and re-layouts  3.73 us (11%)
  between operations  1.33 us (4%)
    ppermute x8, waiting for transfers between devices, move(): lax.ppermute(x, BOTH, [(i * ctx + j, to(i, j)[0] * ctx + to(i, j)[1]) for...  10.7 us
    ppermute x8, starting transfers between devices, move(): lax.ppermute(x, BOTH, [(i * ctx + j, to(i, j)[0] * ctx + to(i, j)[1]) for...  9.63 us
    pallas_call x1, Pallas kernels, body(): pl.pallas_call(functools.partial(loss_kernel, docs, len(blocks)), out_sha...  5.58 us
    unnamed x12, local copies, waits for them, and re-layouts  3.64 us
    pallas_call x1, Pallas kernels, body(): pl.pallas_call(functools.partial(pool_kernel, docs), out_shape=(jax.Shape...  2.27 us
  transfers between devices with their start and end apart: 8, of which 5 were waited for; matrix products, arithmetic and copies ran while one was open for 0% of the time, Pallas kernels for 0%

profile of v1, /device:TPU:0, one launch (start us, length us, event | category | flops | bytes accessed | tf_op | source)
XLA Modules:
  0.0 33.3 jit_solution(15498792660099201641)
XLA Ops:
  0.6 0.0 copy-start
  0.6 1.6 %copy-done = bf16[1,256,4096]{2,1,0:T(8,128)(2,1)S(1)} copy-done((bf16[1,256,4096]{2,1,0:T(8,128)(2,1)S(1)}, bf16[1,256,4096]{2,1,0:T(8,128)(2,1)}, u32[]{:S(2)}) %copy-start) | copy-done | bytes 2097176
  2.2 0.0 copy-start.2
  2.2 0.7 %copy-done.2 = f32[4096]{0:T(1024)S(1)} copy-done((f32[4096]{0:T(1024)S(1)}, f32[4096]{0:T(1024)}, u32[]{:S(2)}) %copy-start.2) | copy-done | bytes 16408
  2.9 0.0 copy-start.4
  2.9 0.7 %copy-done.4 = s32[1,256]{1,0:T(1,128)S(1)} copy-done((s32[1,256]{1,0:T(1,128)S(1)}, s32[1,256]{1,0:T(1,128)}, u32[]{:S(2)}) %copy-start.4) | copy-done | bytes 1048
  3.6 0.0 copy-start.5
  3.6 0.7 %copy-done.5 = s32[2]{0:T(128)S(1)} copy-done((s32[2]{0:T(128)S(1)}, s32[2]{0:T(128)}, u32[]{:S(2)}) %copy-start.5) | copy-done | bytes 32
  4.3 0.0 copy-start.1
  4.3 0.0 copy-start.3
  4.3 2.3 %pool.1 = (f32[8,4224]{1,0:T(8,128)S(1)}, bf16[256,128]{1,0:T(8,128)(2,1)S(1)}, f32[256,128]{1,0:T(8,128)S(1)}) custom-call(s32[2]{0:T(128)S(1)} %copy-done.5, s32[1]{0:T(128)} %bitcast.6.place_ref, s32[1,256]{1,0:T(1,128)S(1)} %copy-done.4, f32[1,4096]{1,0:T(1,128)S(1)} %bitcast.11, bf16[1,256,4096]{2,1,0:T(8,128)(2,1)S(1)} %copy-done), custom_call_target="tpu_custom_call" | custom-call | tf_op jit(solution)/shard_map/pool/pallas_call | solution.py:178
  6.6 0.5 %collective-permute-start = (f32[8,4224]{1,0:T(8,128)S(1)}, f32[8,4224]{1,0:T(8,128)S(1)}, u32[]{:S(2)}, u32[]{:S(2)}) collective-permute-start(f32[8,4224]{1,0:T(8,128)S(1)} %get-tuple-element.9), channel_id=1, source_target_pairs={{0,1},{1,0},{2,3},{3,2},{4,5},{5,4},{6,7},{7,6},{8,9},{9,8},{10,11... | collective-permute-start | bytes 405512 | tf_op jit(solution)/shard_map/ppermute | solution.py:176
  7.1 1.0 %collective-permute-done = f32[8,4224]{1,0:T(8,128)S(1)} collective-permute-done((f32[8,4224]{1,0:T(8,128)S(1)}, f32[8,4224]{1,0:T(8,128)S(1)}, u32[]{:S(2)}, u32[]{:S(2)}) %collective-permute-start) | collective-permute-done | bytes 135200 | tf_op jit(solution)/shard_map/ppermute | solution.py:176
  8.1 2.9 %collective-permute-start.3 = (bf16[8,4224]{1,0:T(8,128)(2,1)S(1)}, bf16[8,4224]{1,0:T(8,128)(2,1)S(1)}, u32[]{:S(2)}, u32[]{:S(2)}) collective-permute-start(bf16[8,4224]{1,0:T(8,128)(2,1)S(1)} %add_convert_fusion.2), channel_id=1, source_target_pairs={{0,2},{1,3},{2,0},{3,1},{4,6},{5,7},{6,4},{7,5},{8,10},{9,11},{10,... | collective-permute-start | bytes 202760 | tf_op jit(solution)/shard_map/ppermute | solution.py:176
  11.0 1.4 %collective-permute-start.2 = (bf16[8,4224]{1,0:T(8,128)(2,1)S(1)}, bf16[8,4224]{1,0:T(8,128)(2,1)S(1)}, u32[]{:S(2)}, u32[]{:S(2)}) collective-permute-start(bf16[8,4224]{1,0:T(8,128)(2,1)S(1)} %add_convert_fusion.2), channel_id=1, source_target_pairs={{0,6},{1,7},{2,4},{3,5},{4,2},{5,3},{6,0},{7,1},{8,14},{9,15},{10,... | collective-permute-start | bytes 202760 | tf_op jit(solution)/shard_map/ppermute | solution.py:176
  12.5 0.1 collective-permute-start.1
  12.6 1.7 %collective-permute-done.3 = bf16[8,4224]{1,0:T(8,128)(2,1)S(1)} collective-permute-done((bf16[8,4224]{1,0:T(8,128)(2,1)S(1)}, bf16[8,4224]{1,0:T(8,128)(2,1)S(1)}, u32[]{:S(2)}, u32[]{:S(2)}) %collective-permute-start.3) | collective-permute-done | bytes 67616 | tf_op jit(solution)/shard_map/ppermute | solution.py:176
  14.3 2.5 %collective-permute-done.2 = bf16[8,4224]{1,0:T(8,128)(2,1)S(1)} collective-permute-done((bf16[8,4224]{1,0:T(8,128)(2,1)S(1)}, bf16[8,4224]{1,0:T(8,128)(2,1)S(1)}, u32[]{:S(2)}, u32[]{:S(2)}) %collective-permute-start.2) | collective-permute-done | bytes 67616 | tf_op jit(solution)/shard_map/ppermute | solution.py:176
  16.8 0.0 collective-permute-done.1
  16.8 0.1 broadcast_select_fusion.2
  16.9 1.6 %collective-permute-start.4 = (bf16[16,4224]{1,0:T(8,128)(2,1)S(1)}, bf16[16,4224]{1,0:T(8,128)(2,1)S(1)}, u32[]{:S(2)}, u32[]{:S(2)}) collective-permute-start(bf16[16,4224]{1,0:T(8,128)(2,1)S(1)} %pad_maximum_fusion.refs_0_), channel_id=1, source_target_pairs={{0,8},{1,17},{2,10},{3,19},{4,12},{5,21},{6,14},{7,23},{8,0},{9,25... | collective-permute-start | bytes 405512 | tf_op jit(solution)/shard_map/ppermute | solution.py:176
  18.6 2.5 %collective-permute-start.6 = (bf16[8,4224]{1,0:T(8,128)(2,1)S(1)}, bf16[8,4224]{1,0:T(8,128)(2,1)S(1)}, u32[]{:S(2)}, u32[]{:S(2)}) collective-permute-start(bf16[8,4224]{1,0:T(8,128)(2,1)S(1)} %get-tuple-element.15), channel_id=1, source_target_pairs={{0,24},{1,25},{2,26},{3,27},{4,28},{5,29},{6,30},{7,31},{8,16},{9,... | collective-permute-start | bytes 202760 | tf_op jit(solution)/shard_map/ppermute | solution.py:176
  21.0 4.4 %collective-permute-done.6 = bf16[8,4224]{1,0:T(8,128)(2,1)S(1)} collective-permute-done((bf16[8,4224]{1,0:T(8,128)(2,1)S(1)}, bf16[8,4224]{1,0:T(8,128)(2,1)S(1)}, u32[]{:S(2)}, u32[]{:S(2)}) %collective-permute-start.6) | collective-permute-done | bytes 67616 | tf_op jit(solution)/shard_map/ppermute | solution.py:176
  25.5 0.0 collective-permute-start.7
  26.1 0.1 stack.23.place_ref
  26.2 0.0 collective-permute-done.4.refs_1_
  26.2 0.5 %collective-permute-start.5 = (bf16[16,4224]{1,0:T(8,128)(2,1)S(1)}, bf16[16,4224]{1,0:T(8,128)(2,1)S(1)}, u32[]{:S(2)}, u32[]{:S(2)}) collective-permute-start(bf16[16,4224]{1,0:T(8,128)(2,1)S(1)} %collective-permute-done.4.refs_1_), channel_id=1, source_target_pairs={{0,1},{1,0},{2,3},{3,2},{4,5},{5,4},{6,7},{7,6},{8,9},{9,8},{10,11... | collective-permute-start | bytes 405512 | tf_op jit(solution)/shard_map/ppermute | solution.py:176
  26.7 0.0 collective-permute-done.7
  26.8 1.0 %collective-permute-done.5.refs_2_ = bf16[16,4224]{1,0:T(8,128)(2,1)S(1)} collective-permute-done((bf16[16,4224]{1,0:T(8,128)(2,1)S(1)}, bf16[16,4224]{1,0:T(8,128)(2,1)S(1)}, u32[]{:S(2)}, u32[]{:S(2)}) %collective-permute-start.5) | collective-permute-done | bytes 135200 | tf_op jit(solution)/shard_map/ppermute | solution.py:176
  27.7 0.0 copy-done.1
  27.7 0.0 copy-done.3
  27.7 5.6 %loss.1 = (bf16[1,256,4096]{2,1,0:T(8,128)(2,1)}, f32[1,4096]{1,0:T(1,128)}, f32[1,1]{1,0:T(1,128)}) custom-call(f32[1]{0:T(128)} %bitcast.10.temp_ref, s32[5]{0:T(128)S(1)} %stack.23.place_ref, bf16[16,4224]{1,0:T(8,128)(2,1)S(1)} %pad_maximum_fusion.refs_0_, bf16[16,4224]{1,0:T(8,128)(2,1)S(1)} %collective-permute-done.4.refs_1_, ...), custom_call_target="tpu_custom_call" | custom-call | tf_op jit(solution)/shard_map/loss/pallas_call | solution.py:223
  (4 shorter events, 0.1 us)
Async XLA Ops:
  0.6 1.6 %copy-start = (bf16[1,256,4096]{2,1,0:T(8,128)(2,1)S(1)}, bf16[1,256,4096]{2,1,0:T(8,128)(2,1)}, u32[]{:S(2)}) copy-start(bf16[1,256,4096]{2,1,0:T(8,128)(2,1)} %refs_7_.1) | copy-start | bytes 6291460
  2.2 0.7 %copy-start.2 = (f32[4096]{0:T(1024)S(1)}, f32[4096]{0:T(1024)}, u32[]{:S(2)}) copy-start(f32[4096]{0:T(1024)} %param.7) | copy-start | bytes 49156
  2.9 0.7 %copy-start.4 = (s32[1,256]{1,0:T(1,128)S(1)}, s32[1,256]{1,0:T(1,128)}, u32[]{:S(2)}) copy-start(s32[1,256]{1,0:T(1,128)} %segments_ref.1) | copy-start | bytes 3076
  3.6 0.7 %copy-start.5 = (s32[2]{0:T(128)S(1)}, s32[2]{0:T(128)}, u32[]{:S(2)}) copy-start(s32[2]{0:T(128)} %positives_ref.1) | copy-start | bytes 28
  4.3 23.4 %copy-start.1 = (bf16[1,256,4096]{2,1,0:T(8,128)(2,1)S(1)}, bf16[1,256,4096]{2,1,0:T(8,128)(2,1)}, u32[]{:S(2)}) copy-start(bf16[1,256,4096]{2,1,0:T(8,128)(2,1)} %refs_7_.1) | copy-start | bytes 6291460
  4.3 23.4 %copy-start.3 = (f32[4096]{0:T(1024)S(1)}, f32[4096]{0:T(1024)}, u32[]{:S(2)}) copy-start(f32[4096]{0:T(1024)} %param.7) | copy-start | bytes 49156
  6.6 1.5 %collective-permute-start = (f32[8,4224]{1,0:T(8,128)S(1)}, f32[8,4224]{1,0:T(8,128)S(1)}, u32[]{:S(2)}, u32[]{:S(2)}) collective-permute-start(f32[8,4224]{1,0:T(8,128)S(1)} %get-tuple-element.9), channel_id=1, source_target_pairs={{0,1},{1,0},{2,3},{3,2},{4,5},{5,4},{6,7},{7,6},{8,9},{9,8},{10,11... | collective-permute-start | bytes 405512 | tf_op jit(solution)/shard_map/ppermute | solution.py:176
  8.1 6.2 %collective-permute-start.3 = (bf16[8,4224]{1,0:T(8,128)(2,1)S(1)}, bf16[8,4224]{1,0:T(8,128)(2,1)S(1)}, u32[]{:S(2)}, u32[]{:S(2)}) collective-permute-start(bf16[8,4224]{1,0:T(8,128)(2,1)S(1)} %add_convert_fusion.2), channel_id=1, source_target_pairs={{0,2},{1,3},{2,0},{3,1},{4,6},{5,7},{6,4},{7,5},{8,10},{9,11},{10,... | collective-permute-start | bytes 202760 | tf_op jit(solution)/shard_map/ppermute | solution.py:176
  11.0 5.8 %collective-permute-start.2 = (bf16[8,4224]{1,0:T(8,128)(2,1)S(1)}, bf16[8,4224]{1,0:T(8,128)(2,1)S(1)}, u32[]{:S(2)}, u32[]{:S(2)}) collective-permute-start(bf16[8,4224]{1,0:T(8,128)(2,1)S(1)} %add_convert_fusion.2), channel_id=1, source_target_pairs={{0,6},{1,7},{2,4},{3,5},{4,2},{5,3},{6,0},{7,1},{8,14},{9,15},{10,... | collective-permute-start | bytes 202760 | tf_op jit(solution)/shard_map/ppermute | solution.py:176
  12.5 4.4 %collective-permute-start.1 = (bf16[8,4224]{1,0:T(8,128)(2,1)S(1)}, bf16[8,4224]{1,0:T(8,128)(2,1)S(1)}, u32[]{:S(2)}, u32[]{:S(2)}) collective-permute-start(bf16[8,4224]{1,0:T(8,128)(2,1)S(1)} %add_convert_fusion.2), channel_id=1, source_target_pairs={{0,4},{1,5},{2,6},{3,7},{4,0},{5,1},{6,2},{7,3},{8,12},{9,13},{10,... | collective-permute-start | bytes 202760 | tf_op jit(solution)/shard_map/ppermute | solution.py:176
  16.9 9.3 %collective-permute-start.4 = (bf16[16,4224]{1,0:T(8,128)(2,1)S(1)}, bf16[16,4224]{1,0:T(8,128)(2,1)S(1)}, u32[]{:S(2)}, u32[]{:S(2)}) collective-permute-start(bf16[16,4224]{1,0:T(8,128)(2,1)S(1)} %pad_maximum_fusion.refs_0_), channel_id=1, source_target_pairs={{0,8},{1,17},{2,10},{3,19},{4,12},{5,21},{6,14},{7,23},{8,0},{9,25... | collective-permute-start | bytes 405512 | tf_op jit(solution)/shard_map/ppermute | solution.py:176
  18.6 6.9 %collective-permute-start.6 = (bf16[8,4224]{1,0:T(8,128)(2,1)S(1)}, bf16[8,4224]{1,0:T(8,128)(2,1)S(1)}, u32[]{:S(2)}, u32[]{:S(2)}) collective-permute-start(bf16[8,4224]{1,0:T(8,128)(2,1)S(1)} %get-tuple-element.15), channel_id=1, source_target_pairs={{0,24},{1,25},{2,26},{3,27},{4,28},{5,29},{6,30},{7,31},{8,16},{9,... | collective-permute-start | bytes 202760 | tf_op jit(solution)/shard_map/ppermute | solution.py:176
  25.5 1.3 %collective-permute-start.7 = (bf16[8,4224]{1,0:T(8,128)(2,1)S(1)}, bf16[8,4224]{1,0:T(8,128)(2,1)S(1)}, u32[]{:S(2)}, u32[]{:S(2)}) collective-permute-start(bf16[8,4224]{1,0:T(8,128)(2,1)S(1)} %collective-permute-done.6), channel_id=1, source_target_pairs={{0,1},{1,0},{2,3},{3,2},{4,5},{5,4},{6,7},{7,6},{8,9},{9,8},{10,11... | collective-permute-start | bytes 202760 | tf_op jit(solution)/shard_map/ppermute | solution.py:176
  26.2 1.5 %collective-permute-start.5 = (bf16[16,4224]{1,0:T(8,128)(2,1)S(1)}, bf16[16,4224]{1,0:T(8,128)(2,1)S(1)}, u32[]{:S(2)}, u32[]{:S(2)}) collective-permute-start(bf16[16,4224]{1,0:T(8,128)(2,1)S(1)} %collective-permute-done.4.refs_1_), channel_id=1, source_target_pairs={{0,1},{1,0},{2,3},{3,2},{4,5},{5,4},{6,7},{7,6},{8,9},{9,8},{10,11... | collective-permute-start | bytes 405512 | tf_op jit(solution)/shard_map/ppermute | solution.py:176

commit v2 on v1

--- a/solution.py
+++ b/solution.py
@@ -26,14 +26,19 @@
     return -(-3 * docs // 16) * 16
 
 
-def pool_kernel(docs, positives_ref, place_ref, segments_ref, gain_ref, hidden_ref, part_ref, weights_ref, square_ref, held, acc, sems):
+def pool_kernel(docs, positives_hbm, segments_hbm, gain_hbm, hidden_ref, part_ref, weights_ref, square_ref, positives_ref, segments_ref, gain_ref, held, acc, sems, small_sems):
     tokens, width = held.shape
     rows = _pieces(tokens, POOL_ROWS)
+    small = []
+    for i, (source, target) in enumerate([(segments_hbm, segments_ref), (gain_hbm, gain_ref), (positives_hbm, positives_ref)]):
+        small.append(pltpu.make_async_copy(source, target, small_sems.at[i]))
+        small[-1].start()
     copies = []
     for at in range(0, tokens, rows):
         copy = pltpu.make_async_copy(hidden_ref.at[0, pl.ds(at, rows)], held.at[pl.ds(at, rows)], sems.at[at // rows])
         copy.start()
         copies.append(copy)
+    small[0].wait()
     segments = segments_ref[...]
     slot = lax.broadcasted_iota(jnp.int32, (128, tokens), 0)
     member_t = jnp.where((slot < 3 * docs) & (slot % docs == segments), 1.0, 0.0)
@@ -56,14 +61,17 @@
             acc[...] = part
         else:
             acc[...] += part
+    small[1].wait()
     part_ref[:, :width] = (acc[:docs, :] + acc[docs:, :]) * gain_ref[...]
     count = jnp.sum(member_t[:docs, :], axis=1, keepdims=True).astype(jnp.int32)
     row = lax.broadcasted_iota(jnp.int32, (docs, EXTRA), 0)
     lane = lax.broadcasted_iota(jnp.int32, (docs, EXTRA), 1)
     own = positives_ref.shape[0]
+    small[2].wait()
+    first = lax.axis_index("ctx") * own
     positive = jnp.zeros((docs, EXTRA), jnp.int32)
     for i in range(own):
-        positive = jnp.where(row == place_ref[0] * own + i, positives_ref[i], positive)
+        positive = jnp.where(row == first + i, positives_ref[i], positive)
     digits = jnp.where(lane == 0, count // BASE, 0)
     digits = jnp.where(lane == 1, count % BASE, digits)
     digits = jnp.where(lane == 2, positive // BASE, digits)
@@ -71,17 +79,16 @@
     part_ref[:, width:] = digits.astype(F32)
 
 
-def loss_kernel(docs, n_blocks, temp_ref, place_ref, *refs):
+def loss_kernel(docs, n_blocks, temp_hbm, place_ref, *refs):
     blocks = refs[:n_blocks]
-    gain_ref, weights_ref, square_ref, hidden_ref, grad_hidden_ref, grad_gain_ref, loss_ref, emb, spare, own_rows, held, out, sems = refs[n_blocks:]
-    tokens, width = held.shape
+    gain_ref, weights_ref, square_ref, held, grad_hidden_ref, grad_gain_ref, loss_ref, temp_ref, emb, spare, own_rows, out, sems = refs[n_blocks:]
+    tokens, width = out.shape
     n = emb.shape[0]
     group = blocks[0].shape[0]
-    load = pltpu.make_async_copy(hidden_ref.at[0], held, sems.at[0])
+    load = pltpu.make_async_copy(temp_hbm, temp_ref, sems.at[0])
     load.start()
     for i, block in enumerate(blocks):
         emb[pl.ds(pl.multiple_of(place_ref[1 + i] * group, group), group), :] = block[...]
-    inv_temp = temp_ref[0]
     gram = lax.dot_general(emb[:, :width], emb[:, :width], (((1,), (1,)), ((), ())), preferred_element_type=F32)
     digits = emb[:, width:].astype(F32)
     digits_t = jnp.transpose(digits)
@@ -95,6 +102,8 @@
     norm_c = lax.rsqrt(jnp.sum(squares, axis=1, keepdims=True) + EPS * count_c * count_c)
     norm_r = lax.rsqrt(jnp.sum(squares, axis=0, keepdims=True) + EPS * count_r * count_r)
     cosine = gram * norm_c * norm_r
+    load.wait()
+    inv_temp = temp_ref[0]
     logits = jnp.where(same, -1e30, cosine * inv_temp)
     top = jnp.max(logits, axis=1, keepdims=True)
     expo = jnp.exp(logits - top)
@@ -111,7 +120,6 @@
     mix_high, own_high = mix.astype(BF16), own.astype(BF16)
     mix_low, own_low = (mix - mix_high.astype(F32)).astype(BF16), (own - own_high.astype(F32)).astype(BF16)
     stack = jnp.concatenate([mix_high.astype(F32), mix_low.astype(F32), own_high.astype(F32), own_low.astype(F32)], axis=0).astype(BF16)
-    load.wait()
     lanes = _pieces(width, LANES)
     spare_rows = spare.shape[0]
     inner = jnp.zeros((tokens, spare_rows), F32)
@@ -128,7 +136,7 @@
             parts.append(jnp.zeros((spare_rows - 3 * docs, lanes), F32))
         part = jnp.concatenate(parts, axis=0).astype(BF16)
         spare[:, at : at + lanes] = part
-        inner += lax.dot_general(held[:, at : at + lanes], part, (((1,), (1,)), ((), ())), preferred_element_type=F32)
+        inner += lax.dot_general(held[0, :, at : at + lanes], part, (((1,), (1,)), ((), ())), preferred_element_type=F32)
     weights = weights_ref[:, :spare_rows]
     pull = jnp.sum(weights.astype(F32) * inner, axis=1, keepdims=True) * square_ref[:, 0:1]
     rows = _pieces(tokens, OUT_ROWS)
@@ -136,7 +144,7 @@
     for at in range(0, tokens, rows):
         for left in range(0, width, lanes):
             spread = jnp.dot(weights[at : at + rows, :], spare[:, left : left + lanes], preferred_element_type=F32)
-            states = held[at : at + rows, left : left + lanes].astype(F32)
+            states = held[0, at : at + rows, left : left + lanes].astype(F32)
             out[at : at + rows, left : left + lanes] = (spread - states * pull[at : at + rows, :]).astype(BF16)
         copy = pltpu.make_async_copy(out.at[pl.ds(at, rows)], grad_hidden_ref.at[0, pl.ds(at, rows)], sems.at[1 + at // rows])
         copy.start()
@@ -153,8 +161,8 @@
     return pl.BlockSpec(memory_space=pltpu.SMEM)
 
 
-def _any():
-    return pl.BlockSpec(memory_space=pl.ANY)
+def _hbm():
+    return pl.BlockSpec(memory_space=pltpu.HBM)
 
 
 def tree_sum(values):
@@ -182,16 +190,20 @@
             jax.ShapeDtypeStruct((tokens, 128), BF16),
             jax.ShapeDtypeStruct((tokens, 128), F32),
         ),
-        in_specs=[_smem(), _smem(), _vmem(), _vmem(), _any()],
+        in_specs=[_hbm()] * 4,
         out_specs=(_vmem(), _vmem(), _vmem()),
         scratch_shapes=[
+            pltpu.SMEM(positives.shape, jnp.int32),
+            pltpu.VMEM((1, tokens), jnp.int32),
+            pltpu.VMEM((1, width), F32),
             pltpu.VMEM((tokens, width), BF16),
             pltpu.VMEM((2 * docs, width), F32),
             pltpu.SemaphoreType.DMA((tokens // rows_in,)),
+            pltpu.SemaphoreType.DMA((3,)),
         ],
         compiler_params=pltpu.CompilerParams(vmem_limit_bytes=VMEM_LIMIT),
         name="pool",
-    )(positives, c.reshape(1), segments, gain, hidden)
+    )(*(pltpu.with_memory_space_constraint(x, pltpu.HBM) for x in (positives, segments, gain, hidden)))
 
     chip = (part + move(part, lambda i, j: (i, j ^ 1))).astype(BF16)
     found = {}
@@ -227,13 +239,13 @@
             jax.ShapeDtypeStruct((1, width), F32),
             jax.ShapeDtypeStruct((1, 1), F32),
         ),
-        in_specs=[_smem(), _smem()] + [_vmem()] * (len(blocks) + 3) + [_any()],
-        out_specs=(_any(), _vmem(), _vmem()),
+        in_specs=[_hbm(), _smem()] + [_vmem()] * (len(blocks) + 4),
+        out_specs=(_hbm(), _vmem(), _vmem()),
         scratch_shapes=[
+            pltpu.SMEM((1,), F32),
             pltpu.VMEM((n, width + EXTRA), BF16),
             pltpu.VMEM((_spare_rows(docs), width), BF16),
             pltpu.VMEM((n, n), F32),
-            pltpu.VMEM((tokens, width), BF16),
             pltpu.VMEM((tokens, width), BF16),
             pltpu.SemaphoreType.DMA((1 + tokens // rows_out,)),
         ],

time: 33.6 us -> 30.2 us (0.90)
  local copies, waits for them, and re-layouts: 3.73 us -> 0.09 us
  Pallas kernels: 7.85 us -> 8.26 us
    unnamed x12 -> x4, local copies, waits for them, and re-layouts: 3.64 us -> 0.01 us
    pallas_call x1, Pallas kernels: 2.27 us -> 2.8 us  [body(): pl.pallas_call(functools.partial(pool_kernel, docs), out_shape=(jax.Shape...]
where the time goes in v2:
time: 30.2 us; the launch traced here: 30.1 us
  waiting for transfers between devices  10.7 us (35%)
  starting transfers between devices  9.63 us (32%)
  Pallas kernels  8.26 us (27%)
  between operations  1.33 us (4%)
    ppermute x8, waiting for transfers between devices, move(): lax.ppermute(x, BOTH, [(i * ctx + j, to(i, j)[0] * ctx + to(i, j)[1]) for...  10.7 us
    ppermute x8, starting transfers between devices, move(): lax.ppermute(x, BOTH, [(i * ctx + j, to(i, j)[0] * ctx + to(i, j)[1]) for...  9.63 us
    pallas_call x1, Pallas kernels, body(): pl.pallas_call(functools.partial(loss_kernel, docs, len(blocks)), out_sha...  5.46 us
    pallas_call x1, Pallas kernels, body(): pl.pallas_call(functools.partial(pool_kernel, docs), out_shape=(jax.Shape...  2.8 us
  transfers between devices with their start and end apart: 8, of which 5 were waited for; matrix products, arithmetic and copies ran while one was open for 0% of the time, Pallas kernels for 0%

profile of v2, /device:TPU:0, one launch (start us, length us, event | category | flops | bytes accessed | tf_op | source)
XLA Modules:
  0.0 30.1 jit_solution(3191593533441310715)
XLA Ops:
  0.6 0.0 copy-start
  0.6 0.0 copy-start.1
  0.7 2.8 %pool.1 = (f32[8,4224]{1,0:T(8,128)S(1)}, bf16[256,128]{1,0:T(8,128)(2,1)S(1)}, f32[256,128]{1,0:T(8,128)S(1)}) custom-call(s32[2]{0:T(128)} %positives_hbm.1, s32[1,256]{1,0:T(1,128)} %segments_hbm.1, f32[1,4096]{1,0:T(1,128)} %bitcast.10, bf16[1,256,4096]{2,1,0:T(8,128)(2,1)} %refs_7_.1), custom_call_target="tpu_custom_call" | custom-call | tf_op jit(solution)/shard_map/pool/pallas_call | solution.py:186
  3.5 0.5 %collective-permute-start = (f32[8,4224]{1,0:T(8,128)S(1)}, f32[8,4224]{1,0:T(8,128)S(1)}, u32[]{:S(2)}, u32[]{:S(2)}) collective-permute-start(f32[8,4224]{1,0:T(8,128)S(1)} %get-tuple-element.9), channel_id=1, source_target_pairs={{0,1},{1,0},{2,3},{3,2},{4,5},{5,4},{6,7},{7,6},{8,9},{9,8},{10,11... | collective-permute-start | bytes 405512 | tf_op jit(solution)/shard_map/ppermute | solution.py:184
  4.0 1.0 %collective-permute-done = f32[8,4224]{1,0:T(8,128)S(1)} collective-permute-done((f32[8,4224]{1,0:T(8,128)S(1)}, f32[8,4224]{1,0:T(8,128)S(1)}, u32[]{:S(2)}, u32[]{:S(2)}) %collective-permute-start) | collective-permute-done | bytes 135200 | tf_op jit(solution)/shard_map/ppermute | solution.py:184
  5.0 2.9 %collective-permute-start.3 = (bf16[8,4224]{1,0:T(8,128)(2,1)S(1)}, bf16[8,4224]{1,0:T(8,128)(2,1)S(1)}, u32[]{:S(2)}, u32[]{:S(2)}) collective-permute-start(bf16[8,4224]{1,0:T(8,128)(2,1)S(1)} %add_convert_fusion.2), channel_id=1, source_target_pairs={{0,2},{1,3},{2,0},{3,1},{4,6},{5,7},{6,4},{7,5},{8,10},{9,11},{10,... | collective-permute-start | bytes 202760 | tf_op jit(solution)/shard_map/ppermute | solution.py:184
  7.9 1.4 %collective-permute-start.2 = (bf16[8,4224]{1,0:T(8,128)(2,1)S(1)}, bf16[8,4224]{1,0:T(8,128)(2,1)S(1)}, u32[]{:S(2)}, u32[]{:S(2)}) collective-permute-start(bf16[8,4224]{1,0:T(8,128)(2,1)S(1)} %add_convert_fusion.2), channel_id=1, source_target_pairs={{0,6},{1,7},{2,4},{3,5},{4,2},{5,3},{6,0},{7,1},{8,14},{9,15},{10,... | collective-permute-start | bytes 202760 | tf_op jit(solution)/shard_map/ppermute | solution.py:184
  9.4 0.1 collective-permute-start.1
  9.5 1.7 %collective-permute-done.3 = bf16[8,4224]{1,0:T(8,128)(2,1)S(1)} collective-permute-done((bf16[8,4224]{1,0:T(8,128)(2,1)S(1)}, bf16[8,4224]{1,0:T(8,128)(2,1)S(1)}, u32[]{:S(2)}, u32[]{:S(2)}) %collective-permute-start.3) | collective-permute-done | bytes 67616 | tf_op jit(solution)/shard_map/ppermute | solution.py:184
  11.2 2.5 %collective-permute-done.2 = bf16[8,4224]{1,0:T(8,128)(2,1)S(1)} collective-permute-done((bf16[8,4224]{1,0:T(8,128)(2,1)S(1)}, bf16[8,4224]{1,0:T(8,128)(2,1)S(1)}, u32[]{:S(2)}, u32[]{:S(2)}) %collective-permute-start.2) | collective-permute-done | bytes 67616 | tf_op jit(solution)/shard_map/ppermute | solution.py:184
  13.7 0.0 collective-permute-done.1
  13.7 0.1 broadcast_select_fusion.2
  13.8 1.6 %collective-permute-start.4 = (bf16[16,4224]{1,0:T(8,128)(2,1)S(1)}, bf16[16,4224]{1,0:T(8,128)(2,1)S(1)}, u32[]{:S(2)}, u32[]{:S(2)}) collective-permute-start(bf16[16,4224]{1,0:T(8,128)(2,1)S(1)} %pad_maximum_fusion.refs_0_), channel_id=1, source_target_pairs={{0,8},{1,17},{2,10},{3,19},{4,12},{5,21},{6,14},{7,23},{8,0},{9,25... | collective-permute-start | bytes 405512 | tf_op jit(solution)/shard_map/ppermute | solution.py:184
  15.4 2.5 %collective-permute-start.6 = (bf16[8,4224]{1,0:T(8,128)(2,1)S(1)}, bf16[8,4224]{1,0:T(8,128)(2,1)S(1)}, u32[]{:S(2)}, u32[]{:S(2)}) collective-permute-start(bf16[8,4224]{1,0:T(8,128)(2,1)S(1)} %get-tuple-element.15), channel_id=1, source_target_pairs={{0,24},{1,25},{2,26},{3,27},{4,28},{5,29},{6,30},{7,31},{8,16},{9,... | collective-permute-start | bytes 202760 | tf_op jit(solution)/shard_map/ppermute | solution.py:184
  17.9 4.4 %collective-permute-done.6 = bf16[8,4224]{1,0:T(8,128)(2,1)S(1)} collective-permute-done((bf16[8,4224]{1,0:T(8,128)(2,1)S(1)}, bf16[8,4224]{1,0:T(8,128)(2,1)S(1)}, u32[]{:S(2)}, u32[]{:S(2)}) %collective-permute-start.6) | collective-permute-done | bytes 67616 | tf_op jit(solution)/shard_map/ppermute | solution.py:184
  22.4 0.0 collective-permute-start.7
  23.0 0.1 stack.23.place_ref
  23.1 0.0 collective-permute-done.4.refs_1_
  23.1 0.5 %collective-permute-start.5 = (bf16[16,4224]{1,0:T(8,128)(2,1)S(1)}, bf16[16,4224]{1,0:T(8,128)(2,1)S(1)}, u32[]{:S(2)}, u32[]{:S(2)}) collective-permute-start(bf16[16,4224]{1,0:T(8,128)(2,1)S(1)} %collective-permute-done.4.refs_1_), channel_id=1, source_target_pairs={{0,1},{1,0},{2,3},{3,2},{4,5},{5,4},{6,7},{7,6},{8,9},{9,8},{10,11... | collective-permute-start | bytes 405512 | tf_op jit(solution)/shard_map/ppermute | solution.py:184
  23.6 0.0 collective-permute-done.7
  23.7 1.0 %collective-permute-done.5.refs_2_ = bf16[16,4224]{1,0:T(8,128)(2,1)S(1)} collective-permute-done((bf16[16,4224]{1,0:T(8,128)(2,1)S(1)}, bf16[16,4224]{1,0:T(8,128)(2,1)S(1)}, u32[]{:S(2)}, u32[]{:S(2)}) %collective-permute-start.5) | collective-permute-done | bytes 135200 | tf_op jit(solution)/shard_map/ppermute | solution.py:184
  24.6 0.0 copy-done
  24.6 0.0 copy-done.1
  24.6 5.5 %loss.1 = (bf16[1,256,4096]{2,1,0:T(8,128)(2,1)}, f32[1,4096]{1,0:T(1,128)}, f32[1,1]{1,0:T(1,128)}) custom-call(f32[1]{0:T(128)} %bitcast.9.temp_hbm, s32[5]{0:T(128)S(1)} %stack.23.place_ref, bf16[16,4224]{1,0:T(8,128)(2,1)S(1)} %pad_maximum_fusion.refs_0_, bf16[16,4224]{1,0:T(8,128)(2,1)S(1)} %collective-permute-done.4.refs_1_, ...), custom_call_target="tpu_custom_call" | custom-call | tf_op jit(solution)/shard_map/loss/pallas_call | solution.py:235
  (4 shorter events, 0.1 us)
Async XLA Ops:
  0.6 24.0 %copy-start = (bf16[1,256,4096]{2,1,0:T(8,128)(2,1)S(1)}, bf16[1,256,4096]{2,1,0:T(8,128)(2,1)}, u32[]{:S(2)}) copy-start(bf16[1,256,4096]{2,1,0:T(8,128)(2,1)} %refs_7_.1) | copy-start | bytes 6291460
  0.6 24.0 %copy-start.1 = (f32[4096]{0:T(1024)S(1)}, f32[4096]{0:T(1024)}, u32[]{:S(2)}) copy-start(f32[4096]{0:T(1024)} %param.7) | copy-start | bytes 49156
  3.5 1.5 %collective-permute-start = (f32[8,4224]{1,0:T(8,128)S(1)}, f32[8,4224]{1,0:T(8,128)S(1)}, u32[]{:S(2)}, u32[]{:S(2)}) collective-permute-start(f32[8,4224]{1,0:T(8,128)S(1)} %get-tuple-element.9), channel_id=1, source_target_pairs={{0,1},{1,0},{2,3},{3,2},{4,5},{5,4},{6,7},{7,6},{8,9},{9,8},{10,11... | collective-permute-start | bytes 405512 | tf_op jit(solution)/shard_map/ppermute | solution.py:184
  5.0 6.2 %collective-permute-start.3 = (bf16[8,4224]{1,0:T(8,128)(2,1)S(1)}, bf16[8,4224]{1,0:T(8,128)(2,1)S(1)}, u32[]{:S(2)}, u32[]{:S(2)}) collective-permute-start(bf16[8,4224]{1,0:T(8,128)(2,1)S(1)} %add_convert_fusion.2), channel_id=1, source_target_pairs={{0,2},{1,3},{2,0},{3,1},{4,6},{5,7},{6,4},{7,5},{8,10},{9,11},{10,... | collective-permute-start | bytes 202760 | tf_op jit(solution)/shard_map/ppermute | solution.py:184
  7.9 5.8 %collective-permute-start.2 = (bf16[8,4224]{1,0:T(8,128)(2,1)S(1)}, bf16[8,4224]{1,0:T(8,128)(2,1)S(1)}, u32[]{:S(2)}, u32[]{:S(2)}) collective-permute-start(bf16[8,4224]{1,0:T(8,128)(2,1)S(1)} %add_convert_fusion.2), channel_id=1, source_target_pairs={{0,6},{1,7},{2,4},{3,5},{4,2},{5,3},{6,0},{7,1},{8,14},{9,15},{10,... | collective-permute-start | bytes 202760 | tf_op jit(solution)/shard_map/ppermute | solution.py:184
  9.4 4.4 %collective-permute-start.1 = (bf16[8,4224]{1,0:T(8,128)(2,1)S(1)}, bf16[8,4224]{1,0:T(8,128)(2,1)S(1)}, u32[]{:S(2)}, u32[]{:S(2)}) collective-permute-start(bf16[8,4224]{1,0:T(8,128)(2,1)S(1)} %add_convert_fusion.2), channel_id=1, source_target_pairs={{0,4},{1,5},{2,6},{3,7},{4,0},{5,1},{6,2},{7,3},{8,12},{9,13},{10,... | collective-permute-start | bytes 202760 | tf_op jit(solution)/shard_map/ppermute | solution.py:184
  13.8 9.3 %collective-permute-start.4 = (bf16[16,4224]{1,0:T(8,128)(2,1)S(1)}, bf16[16,4224]{1,0:T(8,128)(2,1)S(1)}, u32[]{:S(2)}, u32[]{:S(2)}) collective-permute-start(bf16[16,4224]{1,0:T(8,128)(2,1)S(1)} %pad_maximum_fusion.refs_0_), channel_id=1, source_target_pairs={{0,8},{1,17},{2,10},{3,19},{4,12},{5,21},{6,14},{7,23},{8,0},{9,25... | collective-permute-start | bytes 405512 | tf_op jit(solution)/shard_map/ppermute | solution.py:184
  15.4 6.9 %collective-permute-start.6 = (bf16[8,4224]{1,0:T(8,128)(2,1)S(1)}, bf16[8,4224]{1,0:T(8,128)(2,1)S(1)}, u32[]{:S(2)}, u32[]{:S(2)}) collective-permute-start(bf16[8,4224]{1,0:T(8,128)(2,1)S(1)} %get-tuple-element.15), channel_id=1, source_target_pairs={{0,24},{1,25},{2,26},{3,27},{4,28},{5,29},{6,30},{7,31},{8,16},{9,... | collective-permute-start | bytes 202760 | tf_op jit(solution)/shard_map/ppermute | solution.py:184
  22.4 1.3 %collective-permute-start.7 = (bf16[8,4224]{1,0:T(8,128)(2,1)S(1)}, bf16[8,4224]{1,0:T(8,128)(2,1)S(1)}, u32[]{:S(2)}, u32[]{:S(2)}) collective-permute-start(bf16[8,4224]{1,0:T(8,128)(2,1)S(1)} %collective-permute-done.6), channel_id=1, source_target_pairs={{0,1},{1,0},{2,3},{3,2},{4,5},{5,4},{6,7},{7,6},{8,9},{9,8},{10,11... | collective-permute-start | bytes 202760 | tf_op jit(solution)/shard_map/ppermute | solution.py:184
  23.1 1.5 %collective-permute-start.5 = (bf16[16,4224]{1,0:T(8,128)(2,1)S(1)}, bf16[16,4224]{1,0:T(8,128)(2,1)S(1)}, u32[]{:S(2)}, u32[]{:S(2)}) collective-permute-start(bf16[16,4224]{1,0:T(8,128)(2,1)S(1)} %collective-permute-done.4.refs_1_), channel_id=1, source_target_pairs={{0,1},{1,0},{2,3},{3,2},{4,5},{5,4},{6,7},{7,6},{8,9},{9,8},{10,11... | collective-permute-start | bytes 405512 | tf_op jit(solution)/shard_map/ppermute | solution.py:184

commit v3 on v2

v3 whole, which is shorter than its diff:
```python
import functools

import jax
import jax.numpy as jnp
from jax import lax
from jax.experimental import pallas as pl
from jax.experimental.pallas import tpu as pltpu
from jax.sharding import PartitionSpec as P

EPS = 1e-06
EXTRA = 128
BASE = 16
POOL_ROWS = 64
OUT_LANES = 1024
LANES = 256
BOTH = ("dp", "ctx")
VMEM_LIMIT = 32 * 1024 * 1024
F32, BF16 = jnp.float32, jnp.bfloat16


def _pieces(size, want):
    return want if size % want == 0 else size


def pool_kernel(docs, n, *refs):
    hidden_ref, *inputs, part_ref, onehot_ref, side_ref, held = refs[:8]
    segments_ref, gain_ref, positives_ref, acc, sems, small_sems = refs[8:]
    tokens, width = held.shape
    rows = _pieces(tokens, POOL_ROWS)
    small = []
    for i, (source, target) in enumerate(zip(inputs, (segments_ref, gain_ref, positives_ref), strict=True)):
        small.append(pltpu.make_async_copy(source, target, small_sems.at[i]))
        small[-1].start()
    copies = []
    for at in range(0, tokens, rows):
        copy = pltpu.make_async_copy(hidden_ref.at[0, pl.ds(at, rows)], held.at[pl.ds(at, rows)], sems.at[at // rows])
        copy.start()
        copies.append(copy)
    rank = lax.axis_index("dp")
    small[0].wait()
    segments = segments_ref[...]
    member = jnp.where(lax.broadcasted_iota(jnp.int32, (docs, tokens), 0) == segments, 1.0, 0.0)
    count = jnp.sum(member, axis=1, keepdims=True).astype(jnp.int32)
    document = jnp.transpose(jnp.broadcast_to(segments.astype(F32), (128, tokens)))[:, 0:1].astype(jnp.int32) + rank * docs
    lane = lax.broadcasted_iota(jnp.int32, onehot_ref.shape, 1)
    onehot_ref[...] = jnp.where(lax.rem(lane, n) == document, 1.0, 0.0).astype(BF16)
    lane = lax.broadcasted_iota(jnp.int32, (rows, 128), 1)
    for step, copy in enumerate(copies):
        at = step * rows
        copy.wait()
        states = held[at : at + rows, :].astype(F32)
        mean = jnp.sum(states * states, axis=1, keepdims=True) / width
        scale = lax.rsqrt(mean + EPS)
        side_ref[at : at + rows, :] = jnp.where(lane == 0, scale, scale * scale / width)
        scale_t = jnp.transpose(jnp.broadcast_to(scale, (rows, 128)))[:docs, :]
        weight = member[:, at : at + rows] * scale_t
        high = weight.astype(BF16).astype(F32)
        weight = jnp.concatenate([high, weight - high], axis=0).astype(BF16)
        part = jnp.dot(weight, held[at : at + rows, :], preferred_element_type=F32)
        if step == 0:
            acc[...] = part
        else:
            acc[...] += part
    small[1].wait()
    part_ref[:, :width] = (acc[:docs, :] + acc[docs:, :]) * gain_ref[...]
    small[2].wait()
    row = lax.broadcasted_iota(jnp.int32, (docs, EXTRA), 0)
    lane = lax.broadcasted_iota(jnp.int32, (docs, EXTRA), 1)
    own = positives_ref.shape[0]
    first = lax.axis_index("ctx") * own
    positive = jnp.zeros((docs, EXTRA), jnp.int32)
    for i in range(own):
        positive = jnp.where(row == first + i, positives_ref[i], positive)
    digits = jnp.where(lane == 0, count // BASE, 0)
    digits = jnp.where(lane == 1, count % BASE, digits)
    digits = jnp.where(lane == 2, positive // BASE, digits)
    digits = jnp.where(lane == 3, positive % BASE, digits)
    part_ref[:, width:] = digits.astype(F32)


def block_groups(n_blocks, groups):
    core = lax.rem(lax.axis_index("ctx"), 2)
    own = lax.div(lax.axis_index("dp"), 2)
    places = [own]
    for k in range(1, groups - 1, 2):
        places += [own ^ (k + core), own ^ (k + 1 - core)]
    if groups > 1:
        places.append(own ^ (groups - 1))
    return places[:n_blocks]


def _high_low(x):
    high = x.astype(BF16).astype(F32)
    return high, x - high


def loss_kernel(n_blocks, *refs):
    blocks = refs[:n_blocks]
    temp_ref, gain_ref, onehot_ref, side_ref, held, grad_hidden_hbm, grad_gain_hbm, loss_hbm = refs[n_blocks : n_blocks + 8]
    emb, scaled, out, grad_gain, loss, sems = refs[n_blocks + 8 :]
    tokens, width = out.shape
    n = emb.shape[0]
    lanes = _pieces(width, LANES)
    group = blocks[0].shape[0]
    for place, block in zip(block_groups(n_blocks, n // group), blocks, strict=True):
        emb[pl.ds(pl.multiple_of(place * group, group), group), :] = block[...]
    gram = lax.dot_general(emb[:, :width], emb[:, :width], (((1,), (1,)), ((), ())), preferred_element_type=F32)
    digits = emb[:, width:].astype(F32)
    digits_t = jnp.transpose(digits)
    count_c = digits[:, 0:1] * BASE + digits[:, 1:2]
    count_r = digits_t[0:1, :] * BASE + digits_t[1:2, :]
    positive_c = (digits[:, 2:3] * BASE + digits[:, 3:4]).astype(jnp.int32)
    positive_r = (digits_t[2:3, :] * BASE + digits_t[3:4, :]).astype(jnp.int32)
    row = lax.broadcasted_iota(jnp.int32, (n, n), 0)
    column = lax.broadcasted_iota(jnp.int32, (n, n), 1)
    same = row == column

    products = jnp.zeros((tokens, n), F32)
    for at in range(0, width, lanes):
        high, low = _high_low(emb[:, at : at + lanes].astype(F32) * gain_ref[:, at : at + lanes])
        high, low = high.astype(BF16), low.astype(BF16)
        scaled[:n, at : at + lanes] = high
        scaled[n : 2 * n, at : at + lanes] = low
        scaled[2 * n :, at : at + lanes] = high
        products += lax.dot_general(held[:, at : at + lanes], high, (((1,), (1,)), ((), ())), preferred_element_type=F32)

    squares = jnp.where(same, gram, 0.0)
    norm_c = lax.rsqrt(jnp.sum(squares, axis=1, keepdims=True) + EPS * count_c * count_c)
    norm_r = lax.rsqrt(jnp.sum(squares, axis=0, keepdims=True) + EPS * count_r * count_r)
    cosine = gram * norm_c * norm_r
    inv_temp = temp_ref[0]
    logits = jnp.where(same, -1e30, cosine * inv_temp)

    def softmax(axis):
        top = jnp.max(logits, axis=axis, keepdims=True)
        expo = jnp.exp(logits - top)
        total = jnp.sum(expo, axis=axis, keepdims=True)
        return top, expo, total

    top, expo, total = softmax(1)
    _, expo_r, total_r = softmax(0)
    pos_c = jnp.where(column == positive_c, 1.0, 0.0)
    pos_r = jnp.where(row == positive_r, 1.0, 0.0)
    terms = top + jnp.log(total) - jnp.sum(pos_c * logits, axis=1, keepdims=True)
    loss[...] = jnp.sum(terms, axis=0, keepdims=True) / n
    loss_copy = pltpu.make_async_copy(loss, loss_hbm, sems.at[0])
    loss_copy.start()
    gmat = ((expo / total - pos_c) * (inv_temp / n)).astype(BF16).astype(F32)
    gmat_t = ((expo_r / total_r - pos_r) * (inv_temp / n)).astype(BF16).astype(F32)
    both = gmat + gmat_t
    along = jnp.sum(both * cosine, axis=1, keepdims=True)
    mix_high, mix_low = _high_low(norm_c * norm_r * (both - jnp.where(same, along, 0.0)))
    mix = jnp.concatenate([mix_high, mix_low], axis=0).astype(BF16)

    wide = jnp.dot(onehot_ref[...], jnp.concatenate([mix] * 3, axis=1), preferred_element_type=F32) * side_ref[:, 0:1]
    pull = jnp.sum(wide[:, :n] * products, axis=1, keepdims=True) * side_ref[:, 1:2]
    high, low = _high_low(wide)
    wide = jnp.where(lax.broadcasted_iota(jnp.int32, wide.shape, 1) < 2 * n, high, low).astype(BF16)
    copies = [loss_copy]
    chunk = _pieces(width, OUT_LANES)
    for left in range(0, width, chunk):
        for at in range(left, left + chunk, lanes):
            spread = jnp.dot(wide, scaled[:, at : at + lanes], preferred_element_type=F32)
            out[:, at : at + lanes] = (spread - held[:, at : at + lanes].astype(F32) * pull).astype(BF16)
            sums = emb[:, at : at + lanes]
            grads = jnp.dot(mix, sums, preferred_element_type=F32)
            grads = jnp.sum((grads[:n, :] + grads[n:, :]) * sums.astype(F32), axis=0, keepdims=True)
            grad_gain[:, at : at + lanes] = grads / gain_ref[:, at : at + lanes]
        copy = pltpu.make_async_copy(
            out.at[:, pl.ds(left, chunk)], grad_hidden_hbm.at[0, :, pl.ds(left, chunk)], sems.at[2 + left // chunk]
        )
        copy.start()
        copies.append(copy)
    copies.append(pltpu.make_async_copy(grad_gain, grad_gain_hbm, sems.at[1]))
    copies[-1].start()
    for copy in copies:
        copy.wait()


def _vmem():
    return pl.BlockSpec(memory_space=pltpu.VMEM)


def _hbm():
    return pl.BlockSpec(memory_space=pltpu.HBM)


def tree_sum(values):
    while len(values) > 1:
        values = [values[i] + values[i + 1] for i in range(0, len(values), 2)]
    return values[0]


def body(dp, ctx, hidden, segments, gain, inv_temp, positives):
    _, tokens, width = hidden.shape
    docs = positives.shape[0] * ctx
    n = docs * dp
    rows = _pieces(tokens, POOL_ROWS)
    d, c = lax.axis_index("dp"), lax.axis_index("ctx")
    core = lax.rem(c, 2)
    gain = gain.reshape(1, width)

    def move(x, to):
        return lax.ppermute(x, BOTH, [(i * ctx + j, to(i, j)[0] * ctx + to(i, j)[1]) for i in range(dp) for j in range(ctx)])

    part, onehot, side, held = pl.pallas_call(
        functools.partial(pool_kernel, docs, n),
        out_shape=(
            jax.ShapeDtypeStruct((docs, width + EXTRA), F32),
            jax.ShapeDtypeStruct((tokens, 2 * n), BF16),
            jax.ShapeDtypeStruct((tokens, 128), F32),
            jax.ShapeDtypeStruct((tokens, width), BF16),
        ),
        in_specs=[_hbm()] * 4,
        out_specs=[_vmem()] * 4,
        scratch_shapes=[
            pltpu.VMEM((1, tokens), jnp.int32),
            pltpu.VMEM((1, width), F32),
            pltpu.SMEM(positives.shape, jnp.int32),
            pltpu.VMEM((2 * docs, width), F32),
            pltpu.SemaphoreType.DMA((tokens // rows,)),
            pltpu.SemaphoreType.DMA((3,)),
        ],
        compiler_params=pltpu.CompilerParams(vmem_limit_bytes=VMEM_LIMIT),
        name="pool",
    )(*(pltpu.with_memory_space_constraint(x, pltpu.HBM) for x in (hidden, segments, gain, positives)))

    chip = (part + move(part, lambda i, j: (i, j ^ 1))).astype(BF16)
    found = {}
    for dx in range(2):
        for dy in range(ctx // 2):
            found[dx, dy] = chip if (dx, dy) == (0, 0) else move(chip, lambda i, j: (i ^ dx, j ^ (2 * dy)))
    here, there = (tree_sum([found[dx, dy].astype(F32) for dy in range(ctx // 2)]).astype(BF16) for dx in range(2))
    odd = lax.rem(d, 2) == 1
    pair = jnp.concatenate([jnp.where(odd, there, here), jnp.where(odd, here, there)], axis=0)

    groups = dp // 2
    blocks = [pair]

    def swap(x):
        return move(x, lambda i, j: (i, j ^ 1))

    for k in range(1, groups - 1, 2):
        mine = move(pair, lambda i, j: (i ^ (2 * (k + j % 2)), j))
        blocks += [mine, swap(mine)]
    if groups > 1:
        half = move(jnp.where(core == 0, pair[:docs], pair[docs:]), lambda i, j: (i ^ (2 * (groups - 1)), j))
        other = swap(half)
        blocks.append(jnp.concatenate([jnp.where(core == 0, half, other), jnp.where(core == 0, other, half)], axis=0))

    grad_hidden, grad_gain, loss = pl.pallas_call(
        functools.partial(loss_kernel, len(blocks)),
        out_shape=(
            jax.ShapeDtypeStruct((1, tokens, width), BF16),
            jax.ShapeDtypeStruct((1, width), F32),
            jax.ShapeDtypeStruct((1, 1), F32),
        ),
        in_specs=[_vmem()] * len(blocks) + [pl.BlockSpec(memory_space=pltpu.SMEM)] + [_vmem()] * 4,
        out_specs=(_hbm(), _hbm(), _hbm()),
        scratch_shapes=[
            pltpu.VMEM((n, width + EXTRA), BF16),
            pltpu.VMEM((3 * n, width), BF16),
            pltpu.VMEM((tokens, width), BF16),
            pltpu.VMEM((1, width), F32),
            pltpu.VMEM((1, 1), F32),
            pltpu.SemaphoreType.DMA((2 + width // _pieces(width, OUT_LANES),)),
        ],
        compiler_params=pltpu.CompilerParams(vmem_limit_bytes=VMEM_LIMIT),
        name="loss",
    )(*blocks, inv_temp.reshape(1), gain, onehot, side, held)
    return grad_hidden, grad_gain.reshape(width), loss.reshape(())


def solution(mesh):
    return jax.shard_map(
        functools.partial(body, mesh.shape["dp"], mesh.shape["ctx"]),
        mesh=mesh,
        in_specs=(P("dp", "ctx", None), P("dp", "ctx"), P(), P(), P(("dp", "ctx"))),
        out_specs=(P("dp", "ctx", None), P(), P()),
        check_vma=False,
    )
```

time: 30.2 us -> 28.2 us (0.934)
  Pallas kernels: 8.26 us -> 6.24 us
    pallas_call x2, Pallas kernels: 8.26 us -> 6.24 us  [the longest x1 3.41 us: body(): pl.pallas_call(functools.partial(loss_kernel, len(blocks)), out_shape=(ja...]
where the time goes in v3:
time: 28.2 us; the launch traced here: 28 us
  waiting for transfers between devices  10.7 us (38%)
  starting transfers between devices  9.69 us (34%)
  Pallas kernels  6.24 us (22%)
  between operations  1.33 us (5%)
    ppermute x8, waiting for transfers between devices, move(): lax.ppermute(x, BOTH, [(i * ctx + j, to(i, j)[0] * ctx + to(i, j)[1]) for...  10.7 us
    ppermute x8, starting transfers between devices, move(): lax.ppermute(x, BOTH, [(i * ctx + j, to(i, j)[0] * ctx + to(i, j)[1]) for...  9.69 us
    pallas_call x1, Pallas kernels, body(): pl.pallas_call(functools.partial(loss_kernel, len(blocks)), out_shape=(ja...  3.41 us
    pallas_call x1, Pallas kernels, body(): pl.pallas_call(functools.partial(pool_kernel, docs, n), out_shape=(jax.Sh...  2.83 us
  transfers between devices with their start and end apart: 8, of which 5 were waited for; matrix products, arithmetic and copies ran while one was open for 0% of the time, Pallas kernels for 0%

profile of v3, /device:TPU:0, one launch (start us, length us, event | category | flops | bytes accessed | tf_op | source)
XLA Modules:
  0.0 28.0 jit_solution(13052240692986117543)
XLA Ops:
  0.6 0.0 copy-start
  0.6 2.8 %pool.1 = (f32[8,4224]{1,0:T(8,128)S(1)}, bf16[256,128]{1,0:T(8,128)(2,1)S(1)}, f32[256,128]{1,0:T(8,128)S(1)}, bf16[256,4096]{1,0:T(8,128)(2,1)S(1)}) custom-call(bf16[1,256,4096]{2,1,0:T(8,128)(2,1)} %refs_0_.1, s32[1,256]{1,0:T(1,128)} %refs_1_.1, f32[1,4096]{1,0:T(1,128)} %bitcast.5, s32[2]{0:T(128)} %refs_3_.1), custom_call_target="tpu_custom_call" | custom-call | tf_op jit(solution)/shard_map/pool/pallas_call | solution.py:206
  3.5 0.5 %collective-permute-start = (f32[8,4224]{1,0:T(8,128)S(1)}, f32[8,4224]{1,0:T(8,128)S(1)}, u32[]{:S(2)}, u32[]{:S(2)}) collective-permute-start(f32[8,4224]{1,0:T(8,128)S(1)} %get-tuple-element.10), channel_id=1, source_target_pairs={{0,1},{1,0},{2,3},{3,2},{4,5},{5,4},{6,7},{7,6},{8,9},{9,8},{10,11... | collective-permute-start | bytes 405512 | tf_op jit(solution)/shard_map/ppermute | solution.py:204
  4.0 1.0 %collective-permute-done = f32[8,4224]{1,0:T(8,128)S(1)} collective-permute-done((f32[8,4224]{1,0:T(8,128)S(1)}, f32[8,4224]{1,0:T(8,128)S(1)}, u32[]{:S(2)}, u32[]{:S(2)}) %collective-permute-start) | collective-permute-done | bytes 135200 | tf_op jit(solution)/shard_map/ppermute | solution.py:204
  5.0 2.9 %collective-permute-start.3 = (bf16[8,4224]{1,0:T(8,128)(2,1)S(1)}, bf16[8,4224]{1,0:T(8,128)(2,1)S(1)}, u32[]{:S(2)}, u32[]{:S(2)}) collective-permute-start(bf16[8,4224]{1,0:T(8,128)(2,1)S(1)} %add_convert_fusion.2), channel_id=1, source_target_pairs={{0,2},{1,3},{2,0},{3,1},{4,6},{5,7},{6,4},{7,5},{8,10},{9,11},{10,... | collective-permute-start | bytes 202760 | tf_op jit(solution)/shard_map/ppermute | solution.py:204
  7.9 1.4 %collective-permute-start.2 = (bf16[8,4224]{1,0:T(8,128)(2,1)S(1)}, bf16[8,4224]{1,0:T(8,128)(2,1)S(1)}, u32[]{:S(2)}, u32[]{:S(2)}) collective-permute-start(bf16[8,4224]{1,0:T(8,128)(2,1)S(1)} %add_convert_fusion.2), channel_id=1, source_target_pairs={{0,6},{1,7},{2,4},{3,5},{4,2},{5,3},{6,0},{7,1},{8,14},{9,15},{10,... | collective-permute-start | bytes 202760 | tf_op jit(solution)/shard_map/ppermute | solution.py:204
  9.4 0.1 collective-permute-start.1
  9.5 1.7 %collective-permute-done.3 = bf16[8,4224]{1,0:T(8,128)(2,1)S(1)} collective-permute-done((bf16[8,4224]{1,0:T(8,128)(2,1)S(1)}, bf16[8,4224]{1,0:T(8,128)(2,1)S(1)}, u32[]{:S(2)}, u32[]{:S(2)}) %collective-permute-start.3) | collective-permute-done | bytes 67616 | tf_op jit(solution)/shard_map/ppermute | solution.py:204
  11.2 2.5 %collective-permute-done.2 = bf16[8,4224]{1,0:T(8,128)(2,1)S(1)} collective-permute-done((bf16[8,4224]{1,0:T(8,128)(2,1)S(1)}, bf16[8,4224]{1,0:T(8,128)(2,1)S(1)}, u32[]{:S(2)}, u32[]{:S(2)}) %collective-permute-start.2) | collective-permute-done | bytes 67616 | tf_op jit(solution)/shard_map/ppermute | solution.py:204
  13.7 0.0 collective-permute-done.1
  13.8 0.1 broadcast_select_fusion.2
  13.8 1.6 %collective-permute-start.4 = (bf16[16,4224]{1,0:T(8,128)(2,1)S(1)}, bf16[16,4224]{1,0:T(8,128)(2,1)S(1)}, u32[]{:S(2)}, u32[]{:S(2)}) collective-permute-start(bf16[16,4224]{1,0:T(8,128)(2,1)S(1)} %pad_maximum_fusion.refs_0_), channel_id=1, source_target_pairs={{0,8},{1,17},{2,10},{3,19},{4,12},{5,21},{6,14},{7,23},{8,0},{9,25... | collective-permute-start | bytes 405512 | tf_op jit(solution)/shard_map/ppermute | solution.py:204
  15.5 2.5 %collective-permute-start.6 = (bf16[8,4224]{1,0:T(8,128)(2,1)S(1)}, bf16[8,4224]{1,0:T(8,128)(2,1)S(1)}, u32[]{:S(2)}, u32[]{:S(2)}) collective-permute-start(bf16[8,4224]{1,0:T(8,128)(2,1)S(1)} %get-tuple-element.17), channel_id=1, source_target_pairs={{0,24},{1,25},{2,26},{3,27},{4,28},{5,29},{6,30},{7,31},{8,16},{9,... | collective-permute-start | bytes 202760 | tf_op jit(solution)/shard_map/ppermute | solution.py:204
  17.9 4.4 %collective-permute-done.6 = bf16[8,4224]{1,0:T(8,128)(2,1)S(1)} collective-permute-done((bf16[8,4224]{1,0:T(8,128)(2,1)S(1)}, bf16[8,4224]{1,0:T(8,128)(2,1)S(1)}, u32[]{:S(2)}, u32[]{:S(2)}) %collective-permute-start.6) | collective-permute-done | bytes 67616 | tf_op jit(solution)/shard_map/ppermute | solution.py:204
  22.4 0.0 collective-permute-start.7
  23.1 0.0 collective-permute-done.4.refs_1_
  23.1 0.6 %collective-permute-start.5 = (bf16[16,4224]{1,0:T(8,128)(2,1)S(1)}, bf16[16,4224]{1,0:T(8,128)(2,1)S(1)}, u32[]{:S(2)}, u32[]{:S(2)}) collective-permute-start(bf16[16,4224]{1,0:T(8,128)(2,1)S(1)} %collective-permute-done.4.refs_1_), channel_id=1, source_target_pairs={{0,1},{1,0},{2,3},{3,2},{4,5},{5,4},{6,7},{7,6},{8,9},{9,8},{10,11... | collective-permute-start | bytes 405512 | tf_op jit(solution)/shard_map/ppermute | solution.py:204
  23.6 0.0 collective-permute-done.7
  23.7 0.9 %collective-permute-done.5.refs_2_ = bf16[16,4224]{1,0:T(8,128)(2,1)S(1)} collective-permute-done((bf16[16,4224]{1,0:T(8,128)(2,1)S(1)}, bf16[16,4224]{1,0:T(8,128)(2,1)S(1)}, u32[]{:S(2)}, u32[]{:S(2)}) %collective-permute-start.5) | collective-permute-done | bytes 135200 | tf_op jit(solution)/shard_map/ppermute | solution.py:204
  24.6 0.0 copy-done
  24.6 3.4 %loss.1 = (bf16[1,256,4096]{2,1,0:T(8,128)(2,1)}, f32[1,4096]{1,0:T(1,128)}, f32[1,1]{1,0:T(1,128)}) custom-call(bf16[16,4224]{1,0:T(8,128)(2,1)S(1)} %pad_maximum_fusion.refs_0_, bf16[16,4224]{1,0:T(8,128)(2,1)S(1)} %collective-permute-done.4.refs_1_, bf16[16,4224]{1,0:T(8,128)(2,1)S(1)} %collective-permute-done.5.refs_2_, ...), custom_call_target="tpu_custom_call" | custom-call | tf_op jit(solution)/shard_map/loss/pallas_call | solution.py:251
  (4 shorter events, 0.1 us)
Async XLA Ops:
  0.6 24.0 %copy-start = (f32[4096]{0:T(1024)S(1)}, f32[4096]{0:T(1024)}, u32[]{:S(2)}) copy-start(f32[4096]{0:T(1024)} %param.7) | copy-start | bytes 49156
  3.5 1.5 %collective-permute-start = (f32[8,4224]{1,0:T(8,128)S(1)}, f32[8,4224]{1,0:T(8,128)S(1)}, u32[]{:S(2)}, u32[]{:S(2)}) collective-permute-start(f32[8,4224]{1,0:T(8,128)S(1)} %get-tuple-element.10), channel_id=1, source_target_pairs={{0,1},{1,0},{2,3},{3,2},{4,5},{5,4},{6,7},{7,6},{8,9},{9,8},{10,11... | collective-permute-start | bytes 405512 | tf_op jit(solution)/shard_map/ppermute | solution.py:204
  5.0 6.2 %collective-permute-start.3 = (bf16[8,4224]{1,0:T(8,128)(2,1)S(1)}, bf16[8,4224]{1,0:T(8,128)(2,1)S(1)}, u32[]{:S(2)}, u32[]{:S(2)}) collective-permute-start(bf16[8,4224]{1,0:T(8,128)(2,1)S(1)} %add_convert_fusion.2), channel_id=1, source_target_pairs={{0,2},{1,3},{2,0},{3,1},{4,6},{5,7},{6,4},{7,5},{8,10},{9,11},{10,... | collective-permute-start | bytes 202760 | tf_op jit(solution)/shard_map/ppermute | solution.py:204
  7.9 5.8 %collective-permute-start.2 = (bf16[8,4224]{1,0:T(8,128)(2,1)S(1)}, bf16[8,4224]{1,0:T(8,128)(2,1)S(1)}, u32[]{:S(2)}, u32[]{:S(2)}) collective-permute-start(bf16[8,4224]{1,0:T(8,128)(2,1)S(1)} %add_convert_fusion.2), channel_id=1, source_target_pairs={{0,6},{1,7},{2,4},{3,5},{4,2},{5,3},{6,0},{7,1},{8,14},{9,15},{10,... | collective-permute-start | bytes 202760 | tf_op jit(solution)/shard_map/ppermute | solution.py:204
  9.4 4.4 %collective-permute-start.1 = (bf16[8,4224]{1,0:T(8,128)(2,1)S(1)}, bf16[8,4224]{1,0:T(8,128)(2,1)S(1)}, u32[]{:S(2)}, u32[]{:S(2)}) collective-permute-start(bf16[8,4224]{1,0:T(8,128)(2,1)S(1)} %add_convert_fusion.2), channel_id=1, source_target_pairs={{0,4},{1,5},{2,6},{3,7},{4,0},{5,1},{6,2},{7,3},{8,12},{9,13},{10,... | collective-permute-start | bytes 202760 | tf_op jit(solution)/shard_map/ppermute | solution.py:204
  13.8 9.2 %collective-permute-start.4 = (bf16[16,4224]{1,0:T(8,128)(2,1)S(1)}, bf16[16,4224]{1,0:T(8,128)(2,1)S(1)}, u32[]{:S(2)}, u32[]{:S(2)}) collective-permute-start(bf16[16,4224]{1,0:T(8,128)(2,1)S(1)} %pad_maximum_fusion.refs_0_), channel_id=1, source_target_pairs={{0,8},{1,17},{2,10},{3,19},{4,12},{5,21},{6,14},{7,23},{8,0},{9,25... | collective-permute-start | bytes 405512 | tf_op jit(solution)/shard_map/ppermute | solution.py:204
  15.5 6.9 %collective-permute-start.6 = (bf16[8,4224]{1,0:T(8,128)(2,1)S(1)}, bf16[8,4224]{1,0:T(8,128)(2,1)S(1)}, u32[]{:S(2)}, u32[]{:S(2)}) collective-permute-start(bf16[8,4224]{1,0:T(8,128)(2,1)S(1)} %get-tuple-element.17), channel_id=1, source_target_pairs={{0,24},{1,25},{2,26},{3,27},{4,28},{5,29},{6,30},{7,31},{8,16},{9,... | collective-permute-start | bytes 202760 | tf_op jit(solution)/shard_map/ppermute | solution.py:204
  22.4 1.3 %collective-permute-start.7 = (bf16[8,4224]{1,0:T(8,128)(2,1)S(1)}, bf16[8,4224]{1,0:T(8,128)(2,1)S(1)}, u32[]{:S(2)}, u32[]{:S(2)}) collective-permute-start(bf16[8,4224]{1,0:T(8,128)(2,1)S(1)} %collective-permute-done.6), channel_id=1, source_target_pairs={{0,1},{1,0},{2,3},{3,2},{4,5},{5,4},{6,7},{7,6},{8,9},{9,8},{10,11... | collective-permute-start | bytes 202760 | tf_op jit(solution)/shard_map/ppermute | solution.py:204
  23.1 1.6 %collective-permute-start.5 = (bf16[16,4224]{1,0:T(8,128)(2,1)S(1)}, bf16[16,4224]{1,0:T(8,128)(2,1)S(1)}, u32[]{:S(2)}, u32[]{:S(2)}) collective-permute-start(bf16[16,4224]{1,0:T(8,128)(2,1)S(1)} %collective-permute-done.4.refs_1_), channel_id=1, source_target_pairs={{0,1},{1,0},{2,3},{3,2},{4,5},{5,4},{6,7},{7,6},{8,9},{9,8},{10,11... | collective-permute-start | bytes 405512 | tf_op jit(solution)/shard_map/ppermute | solution.py:204

commit v4 on v3

--- a/solution.py
+++ b/solution.py
@@ -10,7 +10,7 @@
 EPS = 1e-06
 EXTRA = 128
 BASE = 16
-POOL_ROWS = 64
+POOL_ROWS = 128
 OUT_LANES = 1024
 LANES = 256
 BOTH = ("dp", "ctx")
@@ -78,17 +78,6 @@
     part_ref[:, width:] = digits.astype(F32)
 
 
-def block_groups(n_blocks, groups):
-    core = lax.rem(lax.axis_index("ctx"), 2)
-    own = lax.div(lax.axis_index("dp"), 2)
-    places = [own]
-    for k in range(1, groups - 1, 2):
-        places += [own ^ (k + core), own ^ (k + 1 - core)]
-    if groups > 1:
-        places.append(own ^ (groups - 1))
-    return places[:n_blocks]
-
-
 def _high_low(x):
     high = x.astype(BF16).astype(F32)
     return high, x - high
@@ -102,8 +91,11 @@
     n = emb.shape[0]
     lanes = _pieces(width, LANES)
     group = blocks[0].shape[0]
-    for place, block in zip(block_groups(n_blocks, n // group), blocks, strict=True):
-        emb[pl.ds(pl.multiple_of(place * group, group), group), :] = block[...]
+    own, others = lax.div(lax.axis_index("dp"), 2), n // group
+    emb[pl.ds(pl.multiple_of(own * group, group), group), :] = blocks[0][...]
+    for k in range(1, others):
+        at = (others - 1 - k) * group
+        emb[pl.ds(pl.multiple_of((own ^ k) * group, group), group), :] = blocks[1][at : at + group, :]
     gram = lax.dot_general(emb[:, :width], emb[:, :width], (((1,), (1,)), ((), ())), preferred_element_type=F32)
     digits = emb[:, width:].astype(F32)
     digits_t = jnp.transpose(digits)
@@ -225,28 +217,30 @@
         name="pool",
     )(*(pltpu.with_memory_space_constraint(x, pltpu.HBM) for x in (hidden, segments, gain, positives)))
 
-    chip = (part + move(part, lambda i, j: (i, j ^ 1))).astype(BF16)
-    found = {}
-    for dx in range(2):
-        for dy in range(ctx // 2):
-            found[dx, dy] = chip if (dx, dy) == (0, 0) else move(chip, lambda i, j: (i ^ dx, j ^ (2 * dy)))
-    here, there = (tree_sum([found[dx, dy].astype(F32) for dy in range(ctx // 2)]).astype(BF16) for dx in range(2))
-    odd = lax.rem(d, 2) == 1
-    pair = jnp.concatenate([jnp.where(odd, there, here), jnp.where(odd, here, there)], axis=0)
-
-    groups = dp // 2
-    blocks = [pair]
-
     def swap(x):
         return move(x, lambda i, j: (i, j ^ 1))
 
-    for k in range(1, groups - 1, 2):
-        mine = move(pair, lambda i, j: (i ^ (2 * (k + j % 2)), j))
-        blocks += [mine, swap(mine)]
-    if groups > 1:
-        half = move(jnp.where(core == 0, pair[:docs], pair[docs:]), lambda i, j: (i ^ (2 * (groups - 1)), j))
-        other = swap(half)
-        blocks.append(jnp.concatenate([jnp.where(core == 0, half, other), jnp.where(core == 0, other, half)], axis=0))
+    chip = (part + swap(part)).astype(BF16)
+    lines = ctx // 2
+    found = []
+    for k in range(lines):
+        own = k + 1 if k + 1 < lines else 1
+        found.append(move(chip, lambda i, j: (i ^ 1, j ^ (2 * k)) if j % 2 else (i, j ^ (2 * own))))
+    terms = [jnp.where(core == 0, left, right) for left, right in zip([chip] + found[:-1], found, strict=True)]
+    block = tree_sum([x.astype(F32) for x in terms]).astype(BF16)
+
+    groups = dp // 2
+    even = lax.rem(core + d, 2) == 0
+
+    def both(mine, theirs):
+        pairs = jnp.stack([jnp.where(even, mine, theirs), jnp.where(even, theirs, mine)], axis=1)
+        return pairs.reshape(-1, width + EXTRA)
+
+    far = [move(block, lambda i, j: (i ^ (2 * k), j)) for k in range(groups - 1, 0, -1)]
+    blocks = [both(block[None], swap(block)[None])]
+    if far:
+        far = jnp.stack(far)
+        blocks.append(both(far, swap(far)))
 
     grad_hidden, grad_gain, loss = pl.pallas_call(
         functools.partial(loss_kernel, len(blocks)),

time: 28.2 us -> 26.4 us (0.936)
  starting transfers between devices: 9.69 us -> 7.91 us
  Pallas kernels: 6.24 us -> 5.77 us
    ppermute x8, starting transfers between devices: 9.69 us -> 7.91 us  [move(): lax.ppermute(x, BOTH, [(i * ctx + j, to(i, j)[0] * ctx + to(i, j)[1]) for...]
    pallas_call x1, Pallas kernels: 2.83 us -> 2.37 us  [body(): pl.pallas_call(functools.partial(pool_kernel, docs, n), out_shape=(jax.Sh...]
  transfers between devices with their start and end apart: 8 -> 8, of which waited for: 5 -> 7; matrix products, arithmetic and copies ran while one was open for 0% -> 0% of each run, Pallas kernels for 0% -> 0%
where the time goes in v4:
time: 26.4 us; the launch traced here: 26.2 us
  waiting for transfers between devices  10.9 us (41%)
  starting transfers between devices  7.91 us (30%)
  Pallas kernels  5.77 us (22%)
  between operations  1.38 us (5%)
    ppermute x8, waiting for transfers between devices, move(): lax.ppermute(x, BOTH, [(i * ctx + j, to(i, j)[0] * ctx + to(i, j)[1]) for...  10.9 us
    ppermute x8, starting transfers between devices, move(): lax.ppermute(x, BOTH, [(i * ctx + j, to(i, j)[0] * ctx + to(i, j)[1]) for...  7.91 us
    pallas_call x1, Pallas kernels, body(): pl.pallas_call(functools.partial(loss_kernel, len(blocks)), out_shape=(ja...  3.4 us
    pallas_call x1, Pallas kernels, body(): pl.pallas_call(functools.partial(pool_kernel, docs, n), out_shape=(jax.Sh...  2.37 us
  transfers between devices with their start and end apart: 8, of which 7 were waited for; matrix products, arithmetic and copies ran while one was open for 0% of the time, Pallas kernels for 0%

profile of v4, /device:TPU:0, one launch (start us, length us, event | category | flops | bytes accessed | tf_op | source)
XLA Modules:
  0.0 26.2 jit_solution(6205591482786886910)
XLA Ops:
  0.6 2.4 %pool.1 = (f32[8,4224]{1,0:T(8,128)S(1)}, bf16[256,128]{1,0:T(8,128)(2,1)S(1)}, f32[256,128]{1,0:T(8,128)S(1)}, bf16[256,4096]{1,0:T(8,128)(2,1)S(1)}) custom-call(bf16[1,256,4096]{2,1,0:T(8,128)(2,1)} %refs_0_.1, s32[1,256]{1,0:T(1,128)} %refs_1_.1, f32[1,4096]{1,0:T(1,128)} %bitcast.20, s32[2]{0:T(128)} %refs_3_.1), custom_call_target="tpu_custom_call" | custom-call | tf_op jit(solution)/shard_map/pool/pallas_call | solution.py:198
  3.0 0.0 copy-start
  3.0 0.5 %collective-permute-start = (f32[8,4224]{1,0:T(8,128)S(1)}, f32[8,4224]{1,0:T(8,128)S(1)}, u32[]{:S(2)}, u32[]{:S(2)}) collective-permute-start(f32[8,4224]{1,0:T(8,128)S(1)} %get-tuple-element.10), channel_id=1, source_target_pairs={{0,1},{1,0},{2,3},{3,2},{4,5},{5,4},{6,7},{7,6},{8,9},{9,8},{10,11... | collective-permute-start | bytes 405512 | tf_op jit(solution)/shard_map/ppermute | solution.py:196
  3.5 1.0 %collective-permute-done = f32[8,4224]{1,0:T(8,128)S(1)} collective-permute-done((f32[8,4224]{1,0:T(8,128)S(1)}, f32[8,4224]{1,0:T(8,128)S(1)}, u32[]{:S(2)}, u32[]{:S(2)}) %collective-permute-start) | collective-permute-done | bytes 135200 | tf_op jit(solution)/shard_map/ppermute | solution.py:196
  4.6 2.9 %collective-permute-start.2 = (bf16[8,4224]{1,0:T(8,128)(2,1)S(1)}, bf16[8,4224]{1,0:T(8,128)(2,1)S(1)}, u32[]{:S(2)}, u32[]{:S(2)}) collective-permute-start(bf16[8,4224]{1,0:T(8,128)(2,1)S(1)} %add_convert_fusion.1), channel_id=1, source_target_pairs={{0,2},{1,7},{2,0},{3,5},{4,6},{5,3},{6,4},{7,1},{8,10},{9,15},{10,... | collective-permute-start | bytes 202760 | tf_op jit(solution)/shard_map/ppermute | solution.py:196
  7.5 0.1 collective-permute-start.1
  7.6 2.9 %collective-permute-done.2 = bf16[8,4224]{1,0:T(8,128)(2,1)S(1)} collective-permute-done((bf16[8,4224]{1,0:T(8,128)(2,1)S(1)}, bf16[8,4224]{1,0:T(8,128)(2,1)S(1)}, u32[]{:S(2)}, u32[]{:S(2)}) %collective-permute-start.2) | collective-permute-done | bytes 67616 | tf_op jit(solution)/shard_map/ppermute | solution.py:196
  10.5 1.3 %collective-permute-done.1 = bf16[8,4224]{1,0:T(8,128)(2,1)S(1)} collective-permute-done((bf16[8,4224]{1,0:T(8,128)(2,1)S(1)}, bf16[8,4224]{1,0:T(8,128)(2,1)S(1)}, u32[]{:S(2)}, u32[]{:S(2)}) %collective-permute-start.1) | collective-permute-done | bytes 67616 | tf_op jit(solution)/shard_map/ppermute | solution.py:196
  11.8 2.7 %collective-permute-start.5 = (bf16[8,4224]{1,0:T(8,128)(2,1)S(1)}, bf16[8,4224]{1,0:T(8,128)(2,1)S(1)}, u32[]{:S(2)}, u32[]{:S(2)}) collective-permute-start(bf16[8,4224]{1,0:T(8,128)(2,1)S(1)} %add_convert_fusion), channel_id=1, source_target_pairs={{0,16},{1,17},{2,18},{3,19},{4,20},{5,21},{6,22},{7,23},{8,24},{9,... | collective-permute-start | bytes 202760 | tf_op jit(solution)/shard_map/ppermute | solution.py:196
  14.5 1.3 %collective-permute-start.4 = (bf16[8,4224]{1,0:T(8,128)(2,1)S(1)}, bf16[8,4224]{1,0:T(8,128)(2,1)S(1)}, u32[]{:S(2)}, u32[]{:S(2)}) collective-permute-start(bf16[8,4224]{1,0:T(8,128)(2,1)S(1)} %add_convert_fusion), channel_id=1, source_target_pairs={{0,24},{1,25},{2,26},{3,27},{4,28},{5,29},{6,30},{7,31},{8,16},{9,... | collective-permute-start | bytes 202760 | tf_op jit(solution)/shard_map/ppermute | solution.py:196
  15.8 0.2 collective-permute-start.6
  16.7 0.1 collective-permute-start.3
  16.8 2.9 %collective-permute-done.5 = bf16[8,4224]{1,0:T(8,128)(2,1)S(1)} collective-permute-done((bf16[8,4224]{1,0:T(8,128)(2,1)S(1)}, bf16[8,4224]{1,0:T(8,128)(2,1)S(1)}, u32[]{:S(2)}, u32[]{:S(2)}) %collective-permute-start.5) | collective-permute-done | bytes 67616 | tf_op jit(solution)/shard_map/ppermute | solution.py:196
  19.6 1.2 %collective-permute-done.4 = bf16[8,4224]{1,0:T(8,128)(2,1)S(1)} collective-permute-done((bf16[8,4224]{1,0:T(8,128)(2,1)S(1)}, bf16[8,4224]{1,0:T(8,128)(2,1)S(1)}, u32[]{:S(2)}, u32[]{:S(2)}) %collective-permute-start.4) | collective-permute-done | bytes 67616 | tf_op jit(solution)/shard_map/ppermute | solution.py:196
  20.9 0.3 %collective-permute-done.6 = bf16[8,4224]{1,0:T(8,128)(2,1)S(1)} collective-permute-done((bf16[8,4224]{1,0:T(8,128)(2,1)S(1)}, bf16[8,4224]{1,0:T(8,128)(2,1)S(1)}, u32[]{:S(2)}, u32[]{:S(2)}) %collective-permute-start.6) | collective-permute-done | bytes 67616 | tf_op jit(solution)/shard_map/ppermute | solution.py:196
  21.2 0.1 collective-permute-start.7
  21.2 0.0 collective-permute-done.3
  21.3 1.4 %collective-permute-done.7 = bf16[3,8,4224]{2,1,0:T(8,128)(2,1)S(1)} collective-permute-done((bf16[3,8,4224]{2,1,0:T(8,128)(2,1)S(1)}, bf16[3,8,4224]{2,1,0:T(8,128)(2,1)S(1)}, u32[]{:S(2)}, u32[]{:S(2)}) %collective-permute-start.7) | collective-permute-done | bytes 202784 | tf_op jit(solution)/shard_map/ppermute | solution.py:196
  22.8 0.0 copy-done
  22.8 3.4 %loss.1 = (bf16[1,256,4096]{2,1,0:T(8,128)(2,1)}, f32[1,4096]{1,0:T(1,128)}, f32[1,1]{1,0:T(1,128)}) custom-call(bf16[16,4224]{1,0:T(8,128)(2,1)S(1)} %maximum_bitcast_fusion.refs_0_, bf16[48,4224]{1,0:T(8,128)(2,1)S(1)} %bitcast.19, f32[1]{0:T(128)} %bitcast.18.refs_2_, f32[1,4096]{1,0:T(1,128)S(1)} %bitcast.21, ...), custom_call_target="tpu_custom_call" | custom-call | tf_op jit(solution)/shard_map/loss/pallas_call | solution.py:245
  (8 shorter events, 0.2 us)
Async XLA Ops:
  3.0 19.8 %copy-start = (f32[4096]{0:T(1024)S(1)}, f32[4096]{0:T(1024)}, u32[]{:S(2)}) copy-start(f32[4096]{0:T(1024)} %param.7) | copy-start | bytes 49156
  3.0 1.5 %collective-permute-start = (f32[8,4224]{1,0:T(8,128)S(1)}, f32[8,4224]{1,0:T(8,128)S(1)}, u32[]{:S(2)}, u32[]{:S(2)}) collective-permute-start(f32[8,4224]{1,0:T(8,128)S(1)} %get-tuple-element.10), channel_id=1, source_target_pairs={{0,1},{1,0},{2,3},{3,2},{4,5},{5,4},{6,7},{7,6},{8,9},{9,8},{10,11... | collective-permute-start | bytes 405512 | tf_op jit(solution)/shard_map/ppermute | solution.py:196
  4.6 5.9 %collective-permute-start.2 = (bf16[8,4224]{1,0:T(8,128)(2,1)S(1)}, bf16[8,4224]{1,0:T(8,128)(2,1)S(1)}, u32[]{:S(2)}, u32[]{:S(2)}) collective-permute-start(bf16[8,4224]{1,0:T(8,128)(2,1)S(1)} %add_convert_fusion.1), channel_id=1, source_target_pairs={{0,2},{1,7},{2,0},{3,5},{4,6},{5,3},{6,4},{7,1},{8,10},{9,15},{10,... | collective-permute-start | bytes 202760 | tf_op jit(solution)/shard_map/ppermute | solution.py:196
  7.5 4.3 %collective-permute-start.1 = (bf16[8,4224]{1,0:T(8,128)(2,1)S(1)}, bf16[8,4224]{1,0:T(8,128)(2,1)S(1)}, u32[]{:S(2)}, u32[]{:S(2)}) collective-permute-start(bf16[8,4224]{1,0:T(8,128)(2,1)S(1)} %add_convert_fusion.1), channel_id=1, source_target_pairs={{0,2},{1,5},{2,0},{3,7},{4,6},{5,1},{6,4},{7,3},{8,10},{9,13},{10,... | collective-permute-start | bytes 202760 | tf_op jit(solution)/shard_map/ppermute | solution.py:196
  11.8 7.8 %collective-permute-start.5 = (bf16[8,4224]{1,0:T(8,128)(2,1)S(1)}, bf16[8,4224]{1,0:T(8,128)(2,1)S(1)}, u32[]{:S(2)}, u32[]{:S(2)}) collective-permute-start(bf16[8,4224]{1,0:T(8,128)(2,1)S(1)} %add_convert_fusion), channel_id=1, source_target_pairs={{0,16},{1,17},{2,18},{3,19},{4,20},{5,21},{6,22},{7,23},{8,24},{9,... | collective-permute-start | bytes 202760 | tf_op jit(solution)/shard_map/ppermute | solution.py:196
  14.5 6.4 %collective-permute-start.4 = (bf16[8,4224]{1,0:T(8,128)(2,1)S(1)}, bf16[8,4224]{1,0:T(8,128)(2,1)S(1)}, u32[]{:S(2)}, u32[]{:S(2)}) collective-permute-start(bf16[8,4224]{1,0:T(8,128)(2,1)S(1)} %add_convert_fusion), channel_id=1, source_target_pairs={{0,24},{1,25},{2,26},{3,27},{4,28},{5,29},{6,30},{7,31},{8,16},{9,... | collective-permute-start | bytes 202760 | tf_op jit(solution)/shard_map/ppermute | solution.py:196
  15.8 5.3 %collective-permute-start.6 = (bf16[8,4224]{1,0:T(8,128)(2,1)S(1)}, bf16[8,4224]{1,0:T(8,128)(2,1)S(1)}, u32[]{:S(2)}, u32[]{:S(2)}) collective-permute-start(bf16[8,4224]{1,0:T(8,128)(2,1)S(1)} %add_convert_fusion), channel_id=1, source_target_pairs={{0,8},{1,9},{2,10},{3,11},{4,12},{5,13},{6,14},{7,15},{8,0},{9,1},... | collective-permute-start | bytes 202760 | tf_op jit(solution)/shard_map/ppermute | solution.py:196
  16.7 4.5 %collective-permute-start.3 = (bf16[8,4224]{1,0:T(8,128)(2,1)S(1)}, bf16[8,4224]{1,0:T(8,128)(2,1)S(1)}, u32[]{:S(2)}, u32[]{:S(2)}) collective-permute-start(bf16[8,4224]{1,0:T(8,128)(2,1)S(1)} %add_convert_fusion), channel_id=1, source_target_pairs={{0,1},{1,0},{2,3},{3,2},{4,5},{5,4},{6,7},{7,6},{8,9},{9,8},{10,11... | collective-permute-start | bytes 202760 | tf_op jit(solution)/shard_map/ppermute | solution.py:196
  21.2 1.5 %collective-permute-start.7 = (bf16[3,8,4224]{2,1,0:T(8,128)(2,1)S(1)}, bf16[3,8,4224]{2,1,0:T(8,128)(2,1)S(1)}, u32[]{:S(2)}, u32[]{:S(2)}) collective-permute-start(bf16[3,8,4224]{2,1,0:T(8,128)(2,1)S(1)} %pad_maximum_fusion.1), channel_id=1, source_target_pairs={{0,1},{1,0},{2,3},{3,2},{4,5},{5,4},{6,7},{7,6},{8,9},{9,8},{10,11... | collective-permute-start | bytes 608264 | tf_op jit(solution)/shard_map/ppermute | solution.py:196

commit v5 on v4

--- a/solution.py
+++ b/solution.py
@@ -11,7 +11,8 @@
 EXTRA = 128
 BASE = 16
 POOL_ROWS = 128
-OUT_LANES = 1024
+POOL_LANES = 1024
+OUT_LANES = 512
 LANES = 256
 BOTH = ("dp", "ctx")
 VMEM_LIMIT = 32 * 1024 * 1024
@@ -22,9 +23,14 @@
     return want if size % want == 0 else size
 
 
+def _high_low(x):
+    high = x.astype(BF16).astype(F32)
+    return high, x - high
+
+
 def pool_kernel(docs, n, *refs):
     hidden_ref, *inputs, part_ref, onehot_ref, side_ref, held = refs[:8]
-    segments_ref, gain_ref, positives_ref, acc, sems, small_sems = refs[8:]
+    segments_ref, gain_ref, positives_ref, sems, small_sems = refs[8:]
     tokens, width = held.shape
     rows = _pieces(tokens, POOL_ROWS)
     small = []
@@ -36,6 +42,7 @@
         copy = pltpu.make_async_copy(hidden_ref.at[0, pl.ds(at, rows)], held.at[pl.ds(at, rows)], sems.at[at // rows])
         copy.start()
         copies.append(copy)
+    weights = []
     rank = lax.axis_index("dp")
     small[0].wait()
     segments = segments_ref[...]
@@ -54,16 +61,14 @@
         side_ref[at : at + rows, :] = jnp.where(lane == 0, scale, scale * scale / width)
         scale_t = jnp.transpose(jnp.broadcast_to(scale, (rows, 128)))[:docs, :]
         weight = member[:, at : at + rows] * scale_t
-        high = weight.astype(BF16).astype(F32)
-        weight = jnp.concatenate([high, weight - high], axis=0).astype(BF16)
-        part = jnp.dot(weight, held[at : at + rows, :], preferred_element_type=F32)
-        if step == 0:
-            acc[...] = part
-        else:
-            acc[...] += part
+        weights.append(jnp.concatenate(_high_low(weight), axis=0).astype(BF16))
     small[1].wait()
-    part_ref[:, :width] = (acc[:docs, :] + acc[docs:, :]) * gain_ref[...]
     small[2].wait()
+    weight = jnp.concatenate(weights, axis=1)
+    lanes = _pieces(width, POOL_LANES)
+    for at in range(0, width, lanes):
+        part = jnp.dot(weight, held[:, at : at + lanes], preferred_element_type=F32)
+        part_ref[:, at : at + lanes] = (part[:docs, :] + part[docs:, :]) * gain_ref[:, at : at + lanes]
     row = lax.broadcasted_iota(jnp.int32, (docs, EXTRA), 0)
     lane = lax.broadcasted_iota(jnp.int32, (docs, EXTRA), 1)
     own = positives_ref.shape[0]
@@ -76,11 +81,6 @@
     digits = jnp.where(lane == 2, positive // BASE, digits)
     digits = jnp.where(lane == 3, positive % BASE, digits)
     part_ref[:, width:] = digits.astype(F32)
-
-
-def _high_low(x):
-    high = x.astype(BF16).astype(F32)
-    return high, x - high
 
 
 def loss_kernel(n_blocks, *refs):
@@ -209,7 +209,6 @@
             pltpu.VMEM((1, tokens), jnp.int32),
             pltpu.VMEM((1, width), F32),
             pltpu.SMEM(positives.shape, jnp.int32),
-            pltpu.VMEM((2 * docs, width), F32),
             pltpu.SemaphoreType.DMA((tokens // rows,)),
             pltpu.SemaphoreType.DMA((3,)),
         ],

time: 26.4 us -> 26.3 us (level)
  no operation moved by 1% of the time
where the time goes in v5:
time: 26.3 us; the launch traced here: 26.2 us
  waiting for transfers between devices  10.9 us (41%)
  starting transfers between devices  7.91 us (30%)
  Pallas kernels  5.72 us (22%)
  between operations  1.38 us (5%)
    ppermute x8, waiting for transfers between devices, move(): lax.ppermute(x, BOTH, [(i * ctx + j, to(i, j)[0] * ctx + to(i, j)[1]) for...  10.9 us
    ppermute x8, starting transfers between devices, move(): lax.ppermute(x, BOTH, [(i * ctx + j, to(i, j)[0] * ctx + to(i, j)[1]) for...  7.91 us
    pallas_call x1, Pallas kernels, body(): pl.pallas_call(functools.partial(loss_kernel, len(blocks)), out_shape=(ja...  3.33 us
    pallas_call x1, Pallas kernels, body(): pl.pallas_call(functools.partial(pool_kernel, docs, n), out_shape=(jax.Sh...  2.39 us
  transfers between devices with their start and end apart: 8, of which 7 were waited for; matrix products, arithmetic and copies ran while one was open for 0% of the time, Pallas kernels for 0%

profile of v5, /device:TPU:0, one launch (start us, length us, event | category | flops | bytes accessed | tf_op | source)
XLA Modules:
  0.0 26.2 jit_solution(3671488848858964373)
XLA Ops:
  0.6 2.4 %pool.1 = (f32[8,4224]{1,0:T(8,128)S(1)}, bf16[256,128]{1,0:T(8,128)(2,1)S(1)}, f32[256,128]{1,0:T(8,128)S(1)}, bf16[256,4096]{1,0:T(8,128)(2,1)S(1)}) custom-call(bf16[1,256,4096]{2,1,0:T(8,128)(2,1)} %refs_0_.1, s32[1,256]{1,0:T(1,128)} %refs_1_.1, f32[1,4096]{1,0:T(1,128)} %bitcast.20, s32[2]{0:T(128)} %refs_3_.1), custom_call_target="tpu_custom_call" | custom-call | tf_op jit(solution)/shard_map/pool/pallas_call | solution.py:198
  3.0 0.0 copy-start
  3.0 0.5 %collective-permute-start = (f32[8,4224]{1,0:T(8,128)S(1)}, f32[8,4224]{1,0:T(8,128)S(1)}, u32[]{:S(2)}, u32[]{:S(2)}) collective-permute-start(f32[8,4224]{1,0:T(8,128)S(1)} %get-tuple-element.10), channel_id=1, source_target_pairs={{0,1},{1,0},{2,3},{3,2},{4,5},{5,4},{6,7},{7,6},{8,9},{9,8},{10,11... | collective-permute-start | bytes 405512 | tf_op jit(solution)/shard_map/ppermute | solution.py:196
  3.6 1.0 %collective-permute-done = f32[8,4224]{1,0:T(8,128)S(1)} collective-permute-done((f32[8,4224]{1,0:T(8,128)S(1)}, f32[8,4224]{1,0:T(8,128)S(1)}, u32[]{:S(2)}, u32[]{:S(2)}) %collective-permute-start) | collective-permute-done | bytes 135200 | tf_op jit(solution)/shard_map/ppermute | solution.py:196
  4.6 2.9 %collective-permute-start.2 = (bf16[8,4224]{1,0:T(8,128)(2,1)S(1)}, bf16[8,4224]{1,0:T(8,128)(2,1)S(1)}, u32[]{:S(2)}, u32[]{:S(2)}) collective-permute-start(bf16[8,4224]{1,0:T(8,128)(2,1)S(1)} %add_convert_fusion.1), channel_id=1, source_target_pairs={{0,2},{1,7},{2,0},{3,5},{4,6},{5,3},{6,4},{7,1},{8,10},{9,15},{10,... | collective-permute-start | bytes 202760 | tf_op jit(solution)/shard_map/ppermute | solution.py:196
  7.5 0.1 collective-permute-start.1
  7.6 2.9 %collective-permute-done.2 = bf16[8,4224]{1,0:T(8,128)(2,1)S(1)} collective-permute-done((bf16[8,4224]{1,0:T(8,128)(2,1)S(1)}, bf16[8,4224]{1,0:T(8,128)(2,1)S(1)}, u32[]{:S(2)}, u32[]{:S(2)}) %collective-permute-start.2) | collective-permute-done | bytes 67616 | tf_op jit(solution)/shard_map/ppermute | solution.py:196
  10.5 1.3 %collective-permute-done.1 = bf16[8,4224]{1,0:T(8,128)(2,1)S(1)} collective-permute-done((bf16[8,4224]{1,0:T(8,128)(2,1)S(1)}, bf16[8,4224]{1,0:T(8,128)(2,1)S(1)}, u32[]{:S(2)}, u32[]{:S(2)}) %collective-permute-start.1) | collective-permute-done | bytes 67616 | tf_op jit(solution)/shard_map/ppermute | solution.py:196
  11.8 2.7 %collective-permute-start.5 = (bf16[8,4224]{1,0:T(8,128)(2,1)S(1)}, bf16[8,4224]{1,0:T(8,128)(2,1)S(1)}, u32[]{:S(2)}, u32[]{:S(2)}) collective-permute-start(bf16[8,4224]{1,0:T(8,128)(2,1)S(1)} %add_convert_fusion), channel_id=1, source_target_pairs={{0,16},{1,17},{2,18},{3,19},{4,20},{5,21},{6,22},{7,23},{8,24},{9,... | collective-permute-start | bytes 202760 | tf_op jit(solution)/shard_map/ppermute | solution.py:196
  14.5 1.3 %collective-permute-start.4 = (bf16[8,4224]{1,0:T(8,128)(2,1)S(1)}, bf16[8,4224]{1,0:T(8,128)(2,1)S(1)}, u32[]{:S(2)}, u32[]{:S(2)}) collective-permute-start(bf16[8,4224]{1,0:T(8,128)(2,1)S(1)} %add_convert_fusion), channel_id=1, source_target_pairs={{0,24},{1,25},{2,26},{3,27},{4,28},{5,29},{6,30},{7,31},{8,16},{9,... | collective-permute-start | bytes 202760 | tf_op jit(solution)/shard_map/ppermute | solution.py:196
  15.8 0.2 collective-permute-start.6
  16.7 0.1 collective-permute-start.3
  16.8 2.9 %collective-permute-done.5 = bf16[8,4224]{1,0:T(8,128)(2,1)S(1)} collective-permute-done((bf16[8,4224]{1,0:T(8,128)(2,1)S(1)}, bf16[8,4224]{1,0:T(8,128)(2,1)S(1)}, u32[]{:S(2)}, u32[]{:S(2)}) %collective-permute-start.5) | collective-permute-done | bytes 67616 | tf_op jit(solution)/shard_map/ppermute | solution.py:196
  19.7 1.2 %collective-permute-done.4 = bf16[8,4224]{1,0:T(8,128)(2,1)S(1)} collective-permute-done((bf16[8,4224]{1,0:T(8,128)(2,1)S(1)}, bf16[8,4224]{1,0:T(8,128)(2,1)S(1)}, u32[]{:S(2)}, u32[]{:S(2)}) %collective-permute-start.4) | collective-permute-done | bytes 67616 | tf_op jit(solution)/shard_map/ppermute | solution.py:196
  20.9 0.3 %collective-permute-done.6 = bf16[8,4224]{1,0:T(8,128)(2,1)S(1)} collective-permute-done((bf16[8,4224]{1,0:T(8,128)(2,1)S(1)}, bf16[8,4224]{1,0:T(8,128)(2,1)S(1)}, u32[]{:S(2)}, u32[]{:S(2)}) %collective-permute-start.6) | collective-permute-done | bytes 67616 | tf_op jit(solution)/shard_map/ppermute | solution.py:196
  21.2 0.1 collective-permute-start.7
  21.3 0.0 collective-permute-done.3
  21.3 1.4 %collective-permute-done.7 = bf16[3,8,4224]{2,1,0:T(8,128)(2,1)S(1)} collective-permute-done((bf16[3,8,4224]{2,1,0:T(8,128)(2,1)S(1)}, bf16[3,8,4224]{2,1,0:T(8,128)(2,1)S(1)}, u32[]{:S(2)}, u32[]{:S(2)}) %collective-permute-start.7) | collective-permute-done | bytes 202784 | tf_op jit(solution)/shard_map/ppermute | solution.py:196
  22.8 0.0 copy-done
  22.8 3.3 %loss.1 = (bf16[1,256,4096]{2,1,0:T(8,128)(2,1)}, f32[1,4096]{1,0:T(1,128)}, f32[1,1]{1,0:T(1,128)}) custom-call(bf16[16,4224]{1,0:T(8,128)(2,1)S(1)} %maximum_bitcast_fusion.refs_0_, bf16[48,4224]{1,0:T(8,128)(2,1)S(1)} %bitcast.19, f32[1]{0:T(128)} %bitcast.18.refs_2_, f32[1,4096]{1,0:T(1,128)S(1)} %bitcast.21, ...), custom_call_target="tpu_custom_call" | custom-call | tf_op jit(solution)/shard_map/loss/pallas_call | solution.py:244
  (8 shorter events, 0.2 us)
Async XLA Ops:
  3.0 19.8 %copy-start = (f32[4096]{0:T(1024)S(1)}, f32[4096]{0:T(1024)}, u32[]{:S(2)}) copy-start(f32[4096]{0:T(1024)} %param.7) | copy-start | bytes 49156
  3.0 1.5 %collective-permute-start = (f32[8,4224]{1,0:T(8,128)S(1)}, f32[8,4224]{1,0:T(8,128)S(1)}, u32[]{:S(2)}, u32[]{:S(2)}) collective-permute-start(f32[8,4224]{1,0:T(8,128)S(1)} %get-tuple-element.10), channel_id=1, source_target_pairs={{0,1},{1,0},{2,3},{3,2},{4,5},{5,4},{6,7},{7,6},{8,9},{9,8},{10,11... | collective-permute-start | bytes 405512 | tf_op jit(solution)/shard_map/ppermute | solution.py:196
  4.6 5.9 %collective-permute-start.2 = (bf16[8,4224]{1,0:T(8,128)(2,1)S(1)}, bf16[8,4224]{1,0:T(8,128)(2,1)S(1)}, u32[]{:S(2)}, u32[]{:S(2)}) collective-permute-start(bf16[8,4224]{1,0:T(8,128)(2,1)S(1)} %add_convert_fusion.1), channel_id=1, source_target_pairs={{0,2},{1,7},{2,0},{3,5},{4,6},{5,3},{6,4},{7,1},{8,10},{9,15},{10,... | collective-permute-start | bytes 202760 | tf_op jit(solution)/shard_map/ppermute | solution.py:196
  7.5 4.3 %collective-permute-start.1 = (bf16[8,4224]{1,0:T(8,128)(2,1)S(1)}, bf16[8,4224]{1,0:T(8,128)(2,1)S(1)}, u32[]{:S(2)}, u32[]{:S(2)}) collective-permute-start(bf16[8,4224]{1,0:T(8,128)(2,1)S(1)} %add_convert_fusion.1), channel_id=1, source_target_pairs={{0,2},{1,5},{2,0},{3,7},{4,6},{5,1},{6,4},{7,3},{8,10},{9,13},{10,... | collective-permute-start | bytes 202760 | tf_op jit(solution)/shard_map/ppermute | solution.py:196
  11.8 7.8 %collective-permute-start.5 = (bf16[8,4224]{1,0:T(8,128)(2,1)S(1)}, bf16[8,4224]{1,0:T(8,128)(2,1)S(1)}, u32[]{:S(2)}, u32[]{:S(2)}) collective-permute-start(bf16[8,4224]{1,0:T(8,128)(2,1)S(1)} %add_convert_fusion), channel_id=1, source_target_pairs={{0,16},{1,17},{2,18},{3,19},{4,20},{5,21},{6,22},{7,23},{8,24},{9,... | collective-permute-start | bytes 202760 | tf_op jit(solution)/shard_map/ppermute | solution.py:196
  14.5 6.4 %collective-permute-start.4 = (bf16[8,4224]{1,0:T(8,128)(2,1)S(1)}, bf16[8,4224]{1,0:T(8,128)(2,1)S(1)}, u32[]{:S(2)}, u32[]{:S(2)}) collective-permute-start(bf16[8,4224]{1,0:T(8,128)(2,1)S(1)} %add_convert_fusion), channel_id=1, source_target_pairs={{0,24},{1,25},{2,26},{3,27},{4,28},{5,29},{6,30},{7,31},{8,16},{9,... | collective-permute-start | bytes 202760 | tf_op jit(solution)/shard_map/ppermute | solution.py:196
  15.8 5.3 %collective-permute-start.6 = (bf16[8,4224]{1,0:T(8,128)(2,1)S(1)}, bf16[8,4224]{1,0:T(8,128)(2,1)S(1)}, u32[]{:S(2)}, u32[]{:S(2)}) collective-permute-start(bf16[8,4224]{1,0:T(8,128)(2,1)S(1)} %add_convert_fusion), channel_id=1, source_target_pairs={{0,8},{1,9},{2,10},{3,11},{4,12},{5,13},{6,14},{7,15},{8,0},{9,1},... | collective-permute-start | bytes 202760 | tf_op jit(solution)/shard_map/ppermute | solution.py:196
  16.7 4.5 %collective-permute-start.3 = (bf16[8,4224]{1,0:T(8,128)(2,1)S(1)}, bf16[8,4224]{1,0:T(8,128)(2,1)S(1)}, u32[]{:S(2)}, u32[]{:S(2)}) collective-permute-start(bf16[8,4224]{1,0:T(8,128)(2,1)S(1)} %add_convert_fusion), channel_id=1, source_target_pairs={{0,1},{1,0},{2,3},{3,2},{4,5},{5,4},{6,7},{7,6},{8,9},{9,8},{10,11... | collective-permute-start | bytes 202760 | tf_op jit(solution)/shard_map/ppermute | solution.py:196
  21.2 1.5 %collective-permute-start.7 = (bf16[3,8,4224]{2,1,0:T(8,128)(2,1)S(1)}, bf16[3,8,4224]{2,1,0:T(8,128)(2,1)S(1)}, u32[]{:S(2)}, u32[]{:S(2)}) collective-permute-start(bf16[3,8,4224]{2,1,0:T(8,128)(2,1)S(1)} %pad_maximum_fusion.1), channel_id=1, source_target_pairs={{0,1},{1,0},{2,3},{3,2},{4,5},{5,4},{6,7},{7,6},{8,9},{9,8},{10,11... | collective-permute-start | bytes 608264 | tf_op jit(solution)/shard_map/ppermute | solution.py:196

commit v6 on v5

--- a/solution.py
+++ b/solution.py
@@ -154,15 +154,16 @@
         for at in range(left, left + chunk, lanes):
             spread = jnp.dot(wide, scaled[:, at : at + lanes], preferred_element_type=F32)
             out[:, at : at + lanes] = (spread - held[:, at : at + lanes].astype(F32) * pull).astype(BF16)
-            sums = emb[:, at : at + lanes]
-            grads = jnp.dot(mix, sums, preferred_element_type=F32)
-            grads = jnp.sum((grads[:n, :] + grads[n:, :]) * sums.astype(F32), axis=0, keepdims=True)
-            grad_gain[:, at : at + lanes] = grads / gain_ref[:, at : at + lanes]
         copy = pltpu.make_async_copy(
             out.at[:, pl.ds(left, chunk)], grad_hidden_hbm.at[0, :, pl.ds(left, chunk)], sems.at[2 + left // chunk]
         )
         copy.start()
         copies.append(copy)
+    for at in range(0, width, lanes):
+        sums = emb[:, at : at + lanes]
+        grads = jnp.dot(mix, sums, preferred_element_type=F32)
+        grads = jnp.sum((grads[:n, :] + grads[n:, :]) * sums.astype(F32), axis=0, keepdims=True)
+        grad_gain[:, at : at + lanes] = grads / gain_ref[:, at : at + lanes]
     copies.append(pltpu.make_async_copy(grad_gain, grad_gain_hbm, sems.at[1]))
     copies[-1].start()
     for copy in copies:

time: 26.3 us -> 26.3 us (level)
  no operation moved by 1% of the time
where the time goes in v6:
time: 26.3 us; the launch traced here: 26.1 us
  waiting for transfers between devices  10.9 us (41%)
  starting transfers between devices  7.91 us (30%)
  Pallas kernels  5.67 us (22%)
  between operations  1.38 us (5%)
    ppermute x8, waiting for transfers between devices, move(): lax.ppermute(x, BOTH, [(i * ctx + j, to(i, j)[0] * ctx + to(i, j)[1]) for...  10.9 us
    ppermute x8, starting transfers between devices, move(): lax.ppermute(x, BOTH, [(i * ctx + j, to(i, j)[0] * ctx + to(i, j)[1]) for...  7.91 us
    pallas_call x1, Pallas kernels, body(): pl.pallas_call(functools.partial(loss_kernel, len(blocks)), out_shape=(ja...  3.29 us
    pallas_call x1, Pallas kernels, body(): pl.pallas_call(functools.partial(pool_kernel, docs, n), out_shape=(jax.Sh...  2.39 us
  transfers between devices with their start and end apart: 8, of which 7 were waited for; matrix products, arithmetic and copies ran while one was open for 0% of the time, Pallas kernels for 0%

profile of v6, /device:TPU:0, one launch (start us, length us, event | category | flops | bytes accessed | tf_op | source)
XLA Modules:
  0.0 26.1 jit_solution(13689611301963561377)
XLA Ops:
  0.6 2.4 %pool.1 = (f32[8,4224]{1,0:T(8,128)S(1)}, bf16[256,128]{1,0:T(8,128)(2,1)S(1)}, f32[256,128]{1,0:T(8,128)S(1)}, bf16[256,4096]{1,0:T(8,128)(2,1)S(1)}) custom-call(bf16[1,256,4096]{2,1,0:T(8,128)(2,1)} %refs_0_.1, s32[1,256]{1,0:T(1,128)} %refs_1_.1, f32[1,4096]{1,0:T(1,128)} %bitcast.20, s32[2]{0:T(128)} %refs_3_.1), custom_call_target="tpu_custom_call" | custom-call | tf_op jit(solution)/shard_map/pool/pallas_call | solution.py:199
  3.0 0.0 copy-start
  3.0 0.5 %collective-permute-start = (f32[8,4224]{1,0:T(8,128)S(1)}, f32[8,4224]{1,0:T(8,128)S(1)}, u32[]{:S(2)}, u32[]{:S(2)}) collective-permute-start(f32[8,4224]{1,0:T(8,128)S(1)} %get-tuple-element.10), channel_id=1, source_target_pairs={{0,1},{1,0},{2,3},{3,2},{4,5},{5,4},{6,7},{7,6},{8,9},{9,8},{10,11... | collective-permute-start | bytes 405512 | tf_op jit(solution)/shard_map/ppermute | solution.py:197
  3.6 1.0 %collective-permute-done = f32[8,4224]{1,0:T(8,128)S(1)} collective-permute-done((f32[8,4224]{1,0:T(8,128)S(1)}, f32[8,4224]{1,0:T(8,128)S(1)}, u32[]{:S(2)}, u32[]{:S(2)}) %collective-permute-start) | collective-permute-done | bytes 135200 | tf_op jit(solution)/shard_map/ppermute | solution.py:197
  4.6 2.9 %collective-permute-start.2 = (bf16[8,4224]{1,0:T(8,128)(2,1)S(1)}, bf16[8,4224]{1,0:T(8,128)(2,1)S(1)}, u32[]{:S(2)}, u32[]{:S(2)}) collective-permute-start(bf16[8,4224]{1,0:T(8,128)(2,1)S(1)} %add_convert_fusion.1), channel_id=1, source_target_pairs={{0,2},{1,7},{2,0},{3,5},{4,6},{5,3},{6,4},{7,1},{8,10},{9,15},{10,... | collective-permute-start | bytes 202760 | tf_op jit(solution)/shard_map/ppermute | solution.py:197
  7.5 0.1 collective-permute-start.1
  7.6 2.9 %collective-permute-done.2 = bf16[8,4224]{1,0:T(8,128)(2,1)S(1)} collective-permute-done((bf16[8,4224]{1,0:T(8,128)(2,1)S(1)}, bf16[8,4224]{1,0:T(8,128)(2,1)S(1)}, u32[]{:S(2)}, u32[]{:S(2)}) %collective-permute-start.2) | collective-permute-done | bytes 67616 | tf_op jit(solution)/shard_map/ppermute | solution.py:197
  10.5 1.3 %collective-permute-done.1 = bf16[8,4224]{1,0:T(8,128)(2,1)S(1)} collective-permute-done((bf16[8,4224]{1,0:T(8,128)(2,1)S(1)}, bf16[8,4224]{1,0:T(8,128)(2,1)S(1)}, u32[]{:S(2)}, u32[]{:S(2)}) %collective-permute-start.1) | collective-permute-done | bytes 67616 | tf_op jit(solution)/shard_map/ppermute | solution.py:197
  11.8 2.7 %collective-permute-start.5 = (bf16[8,4224]{1,0:T(8,128)(2,1)S(1)}, bf16[8,4224]{1,0:T(8,128)(2,1)S(1)}, u32[]{:S(2)}, u32[]{:S(2)}) collective-permute-start(bf16[8,4224]{1,0:T(8,128)(2,1)S(1)} %add_convert_fusion), channel_id=1, source_target_pairs={{0,16},{1,17},{2,18},{3,19},{4,20},{5,21},{6,22},{7,23},{8,24},{9,... | collective-permute-start | bytes 202760 | tf_op jit(solution)/shard_map/ppermute | solution.py:197
  14.5 1.3 %collective-permute-start.4 = (bf16[8,4224]{1,0:T(8,128)(2,1)S(1)}, bf16[8,4224]{1,0:T(8,128)(2,1)S(1)}, u32[]{:S(2)}, u32[]{:S(2)}) collective-permute-start(bf16[8,4224]{1,0:T(8,128)(2,1)S(1)} %add_convert_fusion), channel_id=1, source_target_pairs={{0,24},{1,25},{2,26},{3,27},{4,28},{5,29},{6,30},{7,31},{8,16},{9,... | collective-permute-start | bytes 202760 | tf_op jit(solution)/shard_map/ppermute | solution.py:197
  15.8 0.2 collective-permute-start.6
  16.7 0.1 collective-permute-start.3
  16.8 2.9 %collective-permute-done.5 = bf16[8,4224]{1,0:T(8,128)(2,1)S(1)} collective-permute-done((bf16[8,4224]{1,0:T(8,128)(2,1)S(1)}, bf16[8,4224]{1,0:T(8,128)(2,1)S(1)}, u32[]{:S(2)}, u32[]{:S(2)}) %collective-permute-start.5) | collective-permute-done | bytes 67616 | tf_op jit(solution)/shard_map/ppermute | solution.py:197
  19.7 1.2 %collective-permute-done.4 = bf16[8,4224]{1,0:T(8,128)(2,1)S(1)} collective-permute-done((bf16[8,4224]{1,0:T(8,128)(2,1)S(1)}, bf16[8,4224]{1,0:T(8,128)(2,1)S(1)}, u32[]{:S(2)}, u32[]{:S(2)}) %collective-permute-start.4) | collective-permute-done | bytes 67616 | tf_op jit(solution)/shard_map/ppermute | solution.py:197
  20.9 0.3 %collective-permute-done.6 = bf16[8,4224]{1,0:T(8,128)(2,1)S(1)} collective-permute-done((bf16[8,4224]{1,0:T(8,128)(2,1)S(1)}, bf16[8,4224]{1,0:T(8,128)(2,1)S(1)}, u32[]{:S(2)}, u32[]{:S(2)}) %collective-permute-start.6) | collective-permute-done | bytes 67616 | tf_op jit(solution)/shard_map/ppermute | solution.py:197
  21.2 0.1 collective-permute-start.7
  21.3 0.0 collective-permute-done.3
  21.3 1.4 %collective-permute-done.7 = bf16[3,8,4224]{2,1,0:T(8,128)(2,1)S(1)} collective-permute-done((bf16[3,8,4224]{2,1,0:T(8,128)(2,1)S(1)}, bf16[3,8,4224]{2,1,0:T(8,128)(2,1)S(1)}, u32[]{:S(2)}, u32[]{:S(2)}) %collective-permute-start.7) | collective-permute-done | bytes 202784 | tf_op jit(solution)/shard_map/ppermute | solution.py:197
  22.8 0.0 copy-done
  22.8 3.3 %loss.1 = (bf16[1,256,4096]{2,1,0:T(8,128)(2,1)}, f32[1,4096]{1,0:T(1,128)}, f32[1,1]{1,0:T(1,128)}) custom-call(bf16[16,4224]{1,0:T(8,128)(2,1)S(1)} %maximum_bitcast_fusion.refs_0_, bf16[48,4224]{1,0:T(8,128)(2,1)S(1)} %bitcast.19, f32[1]{0:T(128)} %bitcast.18.refs_2_, f32[1,4096]{1,0:T(1,128)S(1)} %bitcast.21, ...), custom_call_target="tpu_custom_call" | custom-call | tf_op jit(solution)/shard_map/loss/pallas_call | solution.py:245
  (8 shorter events, 0.2 us)
Async XLA Ops:
  3.0 19.8 %copy-start = (f32[4096]{0:T(1024)S(1)}, f32[4096]{0:T(1024)}, u32[]{:S(2)}) copy-start(f32[4096]{0:T(1024)} %param.7) | copy-start | bytes 49156
  3.0 1.5 %collective-permute-start = (f32[8,4224]{1,0:T(8,128)S(1)}, f32[8,4224]{1,0:T(8,128)S(1)}, u32[]{:S(2)}, u32[]{:S(2)}) collective-permute-start(f32[8,4224]{1,0:T(8,128)S(1)} %get-tuple-element.10), channel_id=1, source_target_pairs={{0,1},{1,0},{2,3},{3,2},{4,5},{5,4},{6,7},{7,6},{8,9},{9,8},{10,11... | collective-permute-start | bytes 405512 | tf_op jit(solution)/shard_map/ppermute | solution.py:197
  4.6 5.9 %collective-permute-start.2 = (bf16[8,4224]{1,0:T(8,128)(2,1)S(1)}, bf16[8,4224]{1,0:T(8,128)(2,1)S(1)}, u32[]{:S(2)}, u32[]{:S(2)}) collective-permute-start(bf16[8,4224]{1,0:T(8,128)(2,1)S(1)} %add_convert_fusion.1), channel_id=1, source_target_pairs={{0,2},{1,7},{2,0},{3,5},{4,6},{5,3},{6,4},{7,1},{8,10},{9,15},{10,... | collective-permute-start | bytes 202760 | tf_op jit(solution)/shard_map/ppermute | solution.py:197
  7.5 4.3 %collective-permute-start.1 = (bf16[8,4224]{1,0:T(8,128)(2,1)S(1)}, bf16[8,4224]{1,0:T(8,128)(2,1)S(1)}, u32[]{:S(2)}, u32[]{:S(2)}) collective-permute-start(bf16[8,4224]{1,0:T(8,128)(2,1)S(1)} %add_convert_fusion.1), channel_id=1, source_target_pairs={{0,2},{1,5},{2,0},{3,7},{4,6},{5,1},{6,4},{7,3},{8,10},{9,13},{10,... | collective-permute-start | bytes 202760 | tf_op jit(solution)/shard_map/ppermute | solution.py:197
  11.8 7.8 %collective-permute-start.5 = (bf16[8,4224]{1,0:T(8,128)(2,1)S(1)}, bf16[8,4224]{1,0:T(8,128)(2,1)S(1)}, u32[]{:S(2)}, u32[]{:S(2)}) collective-permute-start(bf16[8,4224]{1,0:T(8,128)(2,1)S(1)} %add_convert_fusion), channel_id=1, source_target_pairs={{0,16},{1,17},{2,18},{3,19},{4,20},{5,21},{6,22},{7,23},{8,24},{9,... | collective-permute-start | bytes 202760 | tf_op jit(solution)/shard_map/ppermute | solution.py:197
  14.5 6.4 %collective-permute-start.4 = (bf16[8,4224]{1,0:T(8,128)(2,1)S(1)}, bf16[8,4224]{1,0:T(8,128)(2,1)S(1)}, u32[]{:S(2)}, u32[]{:S(2)}) collective-permute-start(bf16[8,4224]{1,0:T(8,128)(2,1)S(1)} %add_convert_fusion), channel_id=1, source_target_pairs={{0,24},{1,25},{2,26},{3,27},{4,28},{5,29},{6,30},{7,31},{8,16},{9,... | collective-permute-start | bytes 202760 | tf_op jit(solution)/shard_map/ppermute | solution.py:197
  15.8 5.3 %collective-permute-start.6 = (bf16[8,4224]{1,0:T(8,128)(2,1)S(1)}, bf16[8,4224]{1,0:T(8,128)(2,1)S(1)}, u32[]{:S(2)}, u32[]{:S(2)}) collective-permute-start(bf16[8,4224]{1,0:T(8,128)(2,1)S(1)} %add_convert_fusion), channel_id=1, source_target_pairs={{0,8},{1,9},{2,10},{3,11},{4,12},{5,13},{6,14},{7,15},{8,0},{9,1},... | collective-permute-start | bytes 202760 | tf_op jit(solution)/shard_map/ppermute | solution.py:197
  16.7 4.5 %collective-permute-start.3 = (bf16[8,4224]{1,0:T(8,128)(2,1)S(1)}, bf16[8,4224]{1,0:T(8,128)(2,1)S(1)}, u32[]{:S(2)}, u32[]{:S(2)}) collective-permute-start(bf16[8,4224]{1,0:T(8,128)(2,1)S(1)} %add_convert_fusion), channel_id=1, source_target_pairs={{0,1},{1,0},{2,3},{3,2},{4,5},{5,4},{6,7},{7,6},{8,9},{9,8},{10,11... | collective-permute-start | bytes 202760 | tf_op jit(solution)/shard_map/ppermute | solution.py:197
  21.2 1.5 %collective-permute-start.7 = (bf16[3,8,4224]{2,1,0:T(8,128)(2,1)S(1)}, bf16[3,8,4224]{2,1,0:T(8,128)(2,1)S(1)}, u32[]{:S(2)}, u32[]{:S(2)}) collective-permute-start(bf16[3,8,4224]{2,1,0:T(8,128)(2,1)S(1)} %pad_maximum_fusion.1), channel_id=1, source_target_pairs={{0,1},{1,0},{2,3},{3,2},{4,5},{5,4},{6,7},{7,6},{8,9},{9,8},{10,11... | collective-permute-start | bytes 608264 | tf_op jit(solution)/shard_map/ppermute | solution.py:197
